TPU v7x, 32 devices: a whole 2x2x4 slice. The times are simulated.
32 devices in a mesh: pipe: 2 (over core), dp: 2 (over y), seq: 8 (over z, x).
Axes of the slice: x: 2, y: 2, z: 4, core: 2. Of those that a mesh axis runs over, the one named last changes fastest.
Arguments:
- section_feeds: bfloat16 [2, 3, 2, 1024, 640], P('pipe', None, 'dp', 'seq'), may hold values from -6 to 6
- positions: int32 [3, 2, 1024], P(None, 'dp', 'seq'), may hold values from 0 to 1023, as said below
- w_qkv: bfloat16 [2, 640, 1536], P('pipe', None, ('dp', 'seq')), may hold values from -0.25 to 0.25
- w_out: bfloat16 [2, 1024, 640], P('pipe', ('dp', 'seq')), may hold values from -0.1875 to 0.1875
- w_gate_up: bfloat16 [2, 640, 4096], P('pipe', None, ('dp', 'seq')), may hold values from -0.25 to 0.25
- w_down: bfloat16 [2, 2048, 640], P('pipe', ('dp', 'seq')), may hold values from -0.125 to 0.125
- gains: bfloat16 [2, 3072], P('pipe', ('dp', 'seq')), may hold values from 0.5 to 1.5
Outputs:
- section_ends: bfloat16 [2, 3, 2, 1024, 640], P('pipe', None, 'dp', 'seq')
- grad_qkv: float32 [2, 640, 1536], P('pipe', None, ('dp', 'seq'))
- grad_out: float32 [2, 1024, 640], P('pipe', ('dp', 'seq'))
- grad_gate_up: float32 [2, 640, 4096], P('pipe', None, ('dp', 'seq'))
- grad_down: float32 [2, 2048, 640], P('pipe', ('dp', 'seq'))
- grad_gains: float32 [2, 3072], P('pipe', ('dp', 'seq'))
Inputs may be any that keep to these rules, and one draw needn't show every extreme that they name: `positions`: positions count from 0 at each document's start and rise by one within it. In each micro-batch one sequence, drawn from the seed, is a single document; the other holds up to four.
All inputs are finite; a program needn't handle non-finite values.
Results may differ from a plain program's by a relative error of at most 0.033.
Values may be sent and summed in bfloat16 or wider, within the bound.
A program may use at most 256 MiB of HBM per device.

v0:
```python
import jax
import jax.numpy as jnp
from jax import lax
from jax.sharding import PartitionSpec as P

D = 640
HEADS = 4
HEAD_DIM = 256
FF = 2048
WINDOW = 512


epsilon = 1e-06
negative = -1e30


def passed_along(array, axis, by):
    size = lax.axis_size(axis)
    pairs = [(i, i + by) for i in range(size) if 0 <= i + by < size]
    return lax.ppermute(array, axis, pairs)


def rms_scale(values, scale_gain):
    return (
        values * lax.rsqrt(jnp.mean(values * values, axis=-1, keepdims=True) + epsilon) * scale_gain
    )


def rotate(values, position, rope_base):
    half_size = values.shape[-1] // 2
    frequency = rope_base ** (-2.0 * jnp.arange(half_size, dtype=jnp.float32) / values.shape[-1])
    angles = position.astype(jnp.float32)[:, None] * frequency[None, :]
    cosine = jnp.cos(angles)
    sine_part = jnp.sin(angles)
    front_half = values[..., :half_size]
    back_half = values[..., half_size:]
    return jnp.concatenate(
        [front_half * cosine - back_half * sine_part, back_half * cosine + front_half * sine_part],
        axis=-1,
    )


def geglu(gate_up):
    return jax.nn.gelu(gate_up[:, :FF], approximate=True) * gate_up[:, FF:]


def contract_rows(left, right):
    return lax.dot_general(
        left, right, (((0,), (0,)), ((), ())), preferred_element_type=jnp.float32
    )


def contract_cols(left, right):
    return lax.dot_general(
        left, right, (((1,), (1,)), ((), ())), preferred_element_type=jnp.float32
    )


def split_heads(projected, query_gain, key_gain, position, rope_base):
    row_count = projected.shape[0]
    width = HEADS * HEAD_DIM
    queries = projected[:, :width].reshape(row_count, HEADS, HEAD_DIM).transpose(1, 0, 2)
    queries = rotate(rms_scale(queries, query_gain), position, rope_base).reshape(
        HEADS * row_count, HEAD_DIM
    )
    key_rows = rotate(
        rms_scale(projected[:, width : width + HEAD_DIM], key_gain), position, rope_base
    )
    return (queries, key_rows, projected[:, width + HEAD_DIM :])


def query_layout(position, seq_rank, row_count):
    local_index = jnp.tile(jnp.arange(row_count, dtype=jnp.int32), HEADS)
    return (seq_rank * row_count + local_index, jnp.tile(position, HEADS))


def visibility(query_index, places, window, key_count):
    distance = query_index[:, None] - jnp.arange(key_count, dtype=jnp.int32)[None, :]
    return (distance >= 0) & (distance <= places[:, None]) & (distance < window)


def make_forward_fold(queries, query_index, places, window):
    score_scale = HEAD_DIM ** (-0.5)

    def fold_forward(state_in, key_piece, begin_row):
        top_score, denominator, weighted = state_in
        key_count = key_piece.shape[0]
        key_rows = key_piece[:, :HEAD_DIM]
        value_rows = key_piece[:, HEAD_DIM:]
        scores = contract_cols(queries, key_rows) * score_scale
        visible = visibility(query_index, places, window, key_count)
        scores = jnp.where(visible, scores, negative)
        new_top = jnp.maximum(top_score, jnp.max(scores, axis=1))
        weights = jnp.where(visible, jnp.exp(scores - new_top[:, None]), 0.0)
        denominator = jnp.sum(weights, axis=1)
        weighted = jnp.dot(
            weights.astype(jnp.bfloat16), value_rows, preferred_element_type=jnp.float32
        )
        return (new_top, denominator, weighted)

    return fold_forward


def make_backward_fold(queries, query_index, places, window, logsum, grad_rows, row_delta):
    score_scale = HEAD_DIM ** (-0.5)

    def fold_backward(state_in, key_piece, begin_row):
        key_count = key_piece.shape[0]
        key_rows = key_piece[:, :HEAD_DIM]
        value_rows = key_piece[:, HEAD_DIM:]
        scores = contract_cols(queries, key_rows) * score_scale
        visible = visibility(query_index, places, window, key_count)
        probability = jnp.where(visible, jnp.exp(scores - logsum[:, None]), 0.0)
        grad_probability = contract_cols(grad_rows, value_rows)
        grad_scores = (probability * (grad_probability - row_delta[:, None])).astype(jnp.bfloat16)
        grad_queries = (
            jnp.dot(grad_scores, key_rows, preferred_element_type=jnp.float32) * score_scale
        )
        key_part = contract_rows(grad_scores, queries) * score_scale
        value_part = contract_rows(probability.astype(jnp.bfloat16), grad_rows)
        grad_keys = jnp.concatenate([key_part, value_part], axis=1)
        return (grad_queries, grad_keys)

    return fold_backward


def forward_layer(inputs, position, setting):
    weights, rope_base, window, seq_rank, length = setting
    w_qkv, w_out, w_gate_up, w_down, gains = weights
    row_count = inputs.shape[0]
    normed = rms_scale(inputs, gains[:D]).astype(jnp.bfloat16)
    projected = jnp.dot(normed, w_qkv, preferred_element_type=jnp.float32)
    queries, key_rows, value_rows = split_heads(
        projected, gains[4 * D : 4 * D + HEAD_DIM], gains[4 * D + HEAD_DIM :], position, rope_base
    )
    queries = queries.astype(jnp.bfloat16)
    packed = jnp.concatenate([key_rows, value_rows], axis=1).astype(jnp.bfloat16)
    query_index, places = query_layout(position, seq_rank, row_count)
    fold_forward = make_forward_fold(queries, query_index, places, window)
    total_rows = queries.shape[0]
    start_state = (
        jnp.full((total_rows,), negative, jnp.float32),
        jnp.zeros((total_rows,), jnp.float32),
        jnp.zeros((total_rows, HEAD_DIM), jnp.float32),
    )
    kept_state = {}
    top_score, denominator, weighted = fold_forward(
        start_state, lax.all_gather(packed, "seq", axis=0, tiled=True), jnp.int32(0)
    )
    gathered = weighted / denominator[:, None]
    logsum = top_score + jnp.log(denominator)
    attended = (
        gathered.reshape(HEADS, row_count, HEAD_DIM)
        .transpose(1, 0, 2)
        .reshape(row_count, HEADS * HEAD_DIM)
        .astype(jnp.bfloat16)
    )
    branch = jnp.dot(attended, w_out, preferred_element_type=jnp.float32)
    hidden = inputs + rms_scale(branch, gains[D : 2 * D])
    normed_ffw = rms_scale(hidden, gains[2 * D : 3 * D]).astype(jnp.bfloat16)
    gate_up = jnp.dot(normed_ffw, w_gate_up, preferred_element_type=jnp.float32)
    activated = geglu(gate_up).astype(jnp.bfloat16)
    branch_ffw = jnp.dot(activated, w_down, preferred_element_type=jnp.float32)
    output = hidden + rms_scale(branch_ffw, gains[3 * D : 4 * D])
    kept_state["inputs"] = inputs
    kept_state["position"] = position
    kept_state["normed"] = normed
    kept_state["projected"] = projected
    kept_state["queries"] = queries
    kept_state["packed"] = packed
    kept_state["gathered"] = gathered
    kept_state["logsum"] = logsum
    kept_state["attended"] = attended
    kept_state["branch"] = branch
    kept_state["hidden"] = hidden
    kept_state["normed_ffw"] = normed_ffw
    kept_state["gate_up"] = gate_up
    kept_state["activated"] = activated
    kept_state["branch_ffw"] = branch_ffw
    return (output, kept_state)


def backward_layer(incoming, kept_state, setting):
    weights, rope_base, window, seq_rank, length = setting
    w_qkv, w_out, w_gate_up, w_down, gains = weights
    inputs = kept_state["inputs"]
    position = kept_state["position"]
    row_count = inputs.shape[0]
    unused, pullback = jax.vjp(rms_scale, kept_state["branch_ffw"], gains[3 * D : 4 * D])
    grad_branch_ffw, gain_post_ffw = pullback(incoming)
    grad_branch_ffw = grad_branch_ffw.astype(jnp.bfloat16)
    grad_w_down = contract_rows(kept_state["activated"], grad_branch_ffw)
    grad_activated = contract_cols(grad_branch_ffw, w_down)
    unused, pullback = jax.vjp(geglu, kept_state["gate_up"])
    grad_gate_up = pullback(grad_activated)[0].astype(jnp.bfloat16)
    grad_w_gate_up = contract_rows(kept_state["normed_ffw"], grad_gate_up)
    grad_normed_ffw = contract_cols(grad_gate_up, w_gate_up)
    unused, pullback = jax.vjp(rms_scale, kept_state["hidden"], gains[2 * D : 3 * D])
    grad_hidden, gain_pre_ffw = pullback(grad_normed_ffw)
    grad_hidden = grad_hidden + incoming
    unused, pullback = jax.vjp(rms_scale, kept_state["branch"], gains[D : 2 * D])
    grad_branch, gain_post_attn = pullback(grad_hidden)
    grad_branch = grad_branch.astype(jnp.bfloat16)
    grad_w_out = contract_rows(kept_state["attended"], grad_branch)
    grad_attended = contract_cols(grad_branch, w_out).astype(jnp.bfloat16)
    grad_rows = (
        grad_attended.reshape(row_count, HEADS, HEAD_DIM)
        .transpose(1, 0, 2)
        .reshape(HEADS * row_count, HEAD_DIM)
    )
    row_delta = jnp.sum(grad_rows.astype(jnp.float32) * kept_state["gathered"], axis=1)
    query_index, places = query_layout(position, seq_rank, row_count)
    fold_backward = make_backward_fold(
        kept_state["queries"],
        query_index,
        places,
        window,
        kept_state["logsum"],
        grad_rows,
        row_delta,
    )
    key_store = jnp.zeros((length, 2 * HEAD_DIM), jnp.float32)
    start_state = (jnp.zeros((HEADS * row_count, HEAD_DIM), jnp.float32), key_store)
    grad_queries, grad_keys = fold_backward(
        start_state, lax.all_gather(kept_state["packed"], "seq", axis=0, tiled=True), jnp.int32(0)
    )
    grad_keys = lax.psum_scatter(grad_keys, "seq", scatter_dimension=0, tiled=True)
    unused, pullback = jax.vjp(
        lambda projected, query_gain, key_gain: split_heads(
            projected, query_gain, key_gain, position, rope_base
        ),
        kept_state["projected"],
        gains[4 * D : 4 * D + HEAD_DIM],
        gains[4 * D + HEAD_DIM :],
    )
    grad_projected, gain_query, gain_key = pullback(
        (grad_queries, grad_keys[:, :HEAD_DIM], grad_keys[:, HEAD_DIM:])
    )
    grad_projected = grad_projected.astype(jnp.bfloat16)
    grad_w_qkv = contract_rows(kept_state["normed"], grad_projected)
    grad_normed = contract_cols(grad_projected, w_qkv)
    unused, pullback = jax.vjp(rms_scale, inputs, gains[:D])
    grad_inputs, gain_pre_attn = pullback(grad_normed)
    grad_inputs = grad_inputs + grad_hidden
    gain_grads = jnp.concatenate(
        [gain_pre_attn, gain_post_attn, gain_pre_ffw, gain_post_ffw, gain_query, gain_key]
    )
    return (grad_inputs, (grad_w_qkv, grad_w_out, grad_w_gate_up, grad_w_down, gain_grads))


def on_device(section_feeds, positions, w_qkv, w_out, w_gate_up, w_down, gains):
    gathered_weights = (
        lax.all_gather(w_qkv, ("dp", "seq"), axis=2, tiled=True),
        lax.all_gather(w_out, ("dp", "seq"), axis=1, tiled=True),
        lax.all_gather(w_gate_up, ("dp", "seq"), axis=2, tiled=True),
        lax.all_gather(w_down, ("dp", "seq"), axis=1, tiled=True),
        lax.all_gather(gains, ("dp", "seq"), axis=1, tiled=True),
    )
    weights = (
        gathered_weights[0][0],
        gathered_weights[1][0],
        gathered_weights[2][0],
        gathered_weights[3][0],
        gathered_weights[4][0].astype(jnp.float32),
    )
    leading = lax.axis_index("pipe") == 0
    seq_rank = lax.axis_index("seq")
    feeds = section_feeds[0, :, 0]
    places_all = positions[:, 0]
    micro_count = feeds.shape[0]
    row_count = feeds.shape[1]
    length = row_count * lax.axis_size("seq")
    rope_base = jnp.where(leading, 1000000.0, 10000.0).astype(jnp.float32)
    window = jnp.where(leading, length, WINDOW)
    setting = (weights, rope_base, window, seq_rank, length)
    received = jnp.zeros((row_count, D), jnp.bfloat16)
    saved = []
    outputs = []
    for tick_index in range(micro_count + 1):
        which_batch = jnp.where(leading, min(tick_index, micro_count - 1), max(tick_index - 1, 0))
        feed_rows = jnp.where(leading, feeds[min(tick_index, micro_count - 1)], received)
        position = lax.dynamic_index_in_dim(places_all, which_batch, 0, keepdims=False)
        output, kept_state = forward_layer(feed_rows.astype(jnp.float32), position, setting)
        saved.append(kept_state)
        output = output.astype(jnp.bfloat16)
        if tick_index >= 1:
            outputs.append(output)
        if tick_index < micro_count:
            received = passed_along(output, "pipe", 1)
    totals = tuple((jnp.zeros(matrix.shape, jnp.float32) for matrix in weights))
    returned = jnp.zeros((row_count, D), jnp.bfloat16)
    input_grads = []
    for tick_index in range(micro_count + 1):
        is_valid = jnp.where(leading, tick_index >= 1, tick_index < micro_count)
        kept_state = jax.tree.map(
            lambda early, late: jnp.where(leading, early, late),
            saved[max(tick_index - 1, 0)],
            saved[min(tick_index + 1, micro_count)],
        )
        incoming = jnp.where(leading, returned, feeds[min(tick_index, micro_count - 1)])
        grad_input, gradients = backward_layer(incoming.astype(jnp.float32), kept_state, setting)
        totals = tuple(
            (running + jnp.where(is_valid, fresh, 0.0) for running, fresh in zip(totals, gradients))
        )
        grad_input = grad_input.astype(jnp.bfloat16)
        if tick_index >= 1:
            input_grads.append(grad_input)
        if tick_index < micro_count:
            returned = passed_along(grad_input, "pipe", -1)
    section_end = jnp.where(leading, jnp.stack(input_grads), jnp.stack(outputs))
    reduced = (
        lax.psum_scatter(totals[0][None], ("dp", "seq"), scatter_dimension=2, tiled=True),
        lax.psum_scatter(totals[1][None], ("dp", "seq"), scatter_dimension=1, tiled=True),
        lax.psum_scatter(totals[2][None], ("dp", "seq"), scatter_dimension=2, tiled=True),
        lax.psum_scatter(totals[3][None], ("dp", "seq"), scatter_dimension=1, tiled=True),
        lax.psum_scatter(totals[4][None], ("dp", "seq"), scatter_dimension=1, tiled=True),
    )
    return (section_end[None, :, None], reduced[0], reduced[1], reduced[2], reduced[3], reduced[4])


def solution(mesh):
    in_specs = (
        P("pipe", None, "dp", "seq", None),
        P(None, "dp", "seq"),
        P("pipe", None, ("dp", "seq")),
        P("pipe", ("dp", "seq"), None),
        P("pipe", None, ("dp", "seq")),
        P("pipe", ("dp", "seq"), None),
        P("pipe", ("dp", "seq")),
    )
    out_specs = (
        P("pipe", None, "dp", "seq", None),
        P("pipe", None, ("dp", "seq")),
        P("pipe", ("dp", "seq"), None),
        P("pipe", None, ("dp", "seq")),
        P("pipe", ("dp", "seq"), None),
        P("pipe", ("dp", "seq")),
    )
    return jax.shard_map(
        on_device, mesh=mesh, in_specs=in_specs, out_specs=out_specs, check_vma=False
    )
```

profile of v0, /device:TPU:0, one launch (start us, length us, event | category | flops | bytes accessed | tf_op | source)
XLA Modules:
  0.0 1729.9 jit_solution(12613396460383688243)
XLA Ops:
  11.0 44.1 %all-reduce.36 = bf16[3072]{0:T(1024)(128)(2,1)S(1)} all-reduce(bf16[3072]{0:T(1024)(128)(2,1)S(1)} %dynamic-update-slice), channel_id=1, replica_groups=mesh['pipe'=2,'dp'=2,'seq'=8] {'dp','seq'}, use_global_device_ids=true, to_apply=%add.36 | all-reduce | flops 3072 | bytes 12288
  57.5 16.3 all-gather.13.cloned.1.call-done
  73.8 2.4 fusion.72
  81.3 35.2 %all-gather.15.cloned.1.call-done = bf16[1024,512]{1,0:T(8,128)(2,1)} async-done(((bf16[128,512]{1,0:T(8,128)(2,1)}), bf16[1024,512]{1,0:T(8,128)(2,1)}) %all-gather.15.cloned.1.call-update) | async-done | bytes 1048592 | tf_op jit(solution)/shard_map/all_gather | solution.py:148
  121.7 53.3 %all-gather.17.cloned.1.call-done = bf16[1,1024,640]{2,1,0:T(8,128)(2,1)} async-done(((bf16[1,64,640]{2,1,0:T(8,128)(2,1)}), bf16[1,1024,640]{2,1,0:T(8,128)(2,1)}) %all-gather.17.cloned.1.call-update) | async-done | bytes 1310736 | tf_op jit(solution)/shard_map/all_gather | solution.py:254
  177.9 97.9 %all-gather.19.cloned.1.call-done = bf16[1,640,4096]{2,1,0:T(8,128)(2,1)} async-done(((bf16[1,640,256]{2,1,0:T(8,128)(2,1)}), bf16[1,640,4096]{2,1,0:T(8,128)(2,1)}) %all-gather.19.cloned.1.call-update) | async-done | bytes 5242896 | tf_op jit(solution)/shard_map/all_gather | solution.py:255
  275.8 3.5 fusion.14
  281.0 59.6 %all-gather.21.cloned.1.call-done = bf16[1,2048,640]{2,1,0:T(8,128)(2,1)} async-done(((bf16[1,128,640]{2,1,0:T(8,128)(2,1)}), bf16[1,2048,640]{2,1,0:T(8,128)(2,1)}) %all-gather.21.cloned.1.call-update) | async-done | bytes 2621456 | tf_op jit(solution)/shard_map/all_gather | solution.py:256
  340.6 2.5 multiply_reduce_fusion.53
  353.7 34.4 %all-gather.23.cloned.1.call-done = bf16[1024,512]{1,0:T(8,128)(2,1)} async-done(((bf16[128,512]{1,0:T(8,128)(2,1)}), bf16[1024,512]{1,0:T(8,128)(2,1)}) %all-gather.23.cloned.1.call-update) | async-done | bytes 1048592 | tf_op jit(solution)/shard_map/all_gather | solution.py:148
  391.9 2.1 broadcast_select_fusion.11
  399.0 3.6 fusion.12
  402.9 2.1 copy-done.1
  418.3 2.1 reshape.1895
  424.8 29.0 %all-gather.27.cloned.1.call-done = bf16[1024,512]{1,0:T(8,128)(2,1)} async-done(((bf16[128,512]{1,0:T(8,128)(2,1)}), bf16[1024,512]{1,0:T(8,128)(2,1)}) %all-gather.27.cloned.1.call-update) | async-done | bytes 1048592 | tf_op jit(solution)/shard_map/all_gather | solution.py:148
  453.8 2.1 fusion.76
  457.6 2.1 broadcast_select_fusion.10
  465.4 3.5 fusion.10
  469.3 2.1 copy-done.2
  475.9 2.5 broadcast_select_fusion.4
  485.9 2.1 reshape.1906
  492.5 27.8 %all-gather.33.cloned.1.call-done = bf16[1024,512]{1,0:T(8,128)(2,1)} async-done(((bf16[128,512]{1,0:T(8,128)(2,1)}), bf16[1024,512]{1,0:T(8,128)(2,1)}) %all-gather.33.cloned.1.call-update) | async-done | bytes 1048592 | tf_op jit(solution)/shard_map/all_gather | solution.py:148
  520.4 2.1 fusion.77
  523.8 2.3 broadcast_select_fusion.9
  529.5 3.2 multiply_reduce_fusion.44
  534.3 7.6 broadcast_select_fusion
  543.3 2.4 multiply_reduce_fusion.13
  548.9 12.6 all-gather.29.cloned.1.call-done
  561.5 2.2 exponential_select_fusion.3
  570.5 2.1 reshape.1899
  579.5 3.1 multiply_reduce_fusion.30
  585.9 16.5 all-gather.25.cloned.1.call-done
  602.4 3.5 exponential_select_fusion.4
  605.9 66.7 %reduce-scatter.11.cloned.1.call-done = f32[128,512]{1,0:T(8,128)} async-done(((f32[1024,512]{1,0:T(8,128)}), f32[128,512]{1,0:T(8,128)}) %reduce-scatter.11.cloned.1.call-update) | async-done | bytes 262160 | tf_op jit(solution)/shard_map/reduce_scatter | solution.py:227
  676.6 2.2 fusion.239
  693.8 2.4 multiply_reduce_fusion.10
  706.9 2.1 reshape.1904
  715.0 3.6 exponential_select_fusion.1
  719.9 64.0 %reduce-scatter.13.cloned.1.call-done = f32[128,512]{1,0:T(8,128)} async-done(((f32[1024,512]{1,0:T(8,128)}), f32[128,512]{1,0:T(8,128)}) %reduce-scatter.13.cloned.1.call-update) | async-done | bytes 262160 | tf_op jit(solution)/shard_map/reduce_scatter | solution.py:227
  788.0 2.1 fusion.235
  805.2 2.4 multiply_reduce_fusion.7
  818.2 2.1 reshape.1910
  823.7 2.1 reshape.1915
  832.5 3.6 exponential_select_fusion
  837.4 57.8 %reduce-scatter.15.cloned.1.call-done = f32[128,512]{1,0:T(8,128)} async-done(((f32[1024,512]{1,0:T(8,128)}), f32[128,512]{1,0:T(8,128)}) %reduce-scatter.15.cloned.1.call-update) | async-done | bytes 262160 | tf_op jit(solution)/shard_map/reduce_scatter | solution.py:227
  899.2 2.1 fusion.229
  917.3 2.4 multiply_reduce_fusion.4
  931.9 3.7 fusion.330
  939.3 2.7 fusion.328
  942.8 2.8 fusion.326
  946.9 47.1 %reduce-scatter.17.cloned.1.call-done = f32[128,512]{1,0:T(8,128)} async-done(((f32[1024,512]{1,0:T(8,128)}), f32[128,512]{1,0:T(8,128)}) %reduce-scatter.17.cloned.1.call-update) | async-done | bytes 262160 | tf_op jit(solution)/shard_map/reduce_scatter | solution.py:227
  1008.6 6.3 add_bitcast_fusion.2
  1014.9 9.0 copy.203
  1032.3 2.3 add_bitcast_fusion.3
  1038.8 3.7 add_bitcast_fusion.1
  1044.1 6.5 fusion.323
  1050.6 5.4 fusion.321
  1056.1 5.4 fusion.319
  1061.6 12.5 add_bitcast_fusion
  1076.4 55.9 %reduce-scatter.25.cloned.1.call-done = f32[192,1]{1,0:T(8,128)} async-done(((f32[3072,1]{1,0:T(8,128)}), f32[192,1]{1,0:T(8,128)}) %reduce-scatter.25.cloned.1.call-update) | async-done | bytes 784
  1133.8 165.7 %all-reduce.40.cloned.1.call-done = f32[1,640,1536]{1,0,2:T(1,128)} async-done(((f32[1,640,1536]{1,0,2:T(1,128)}), f32[1,640,1536]{1,0,2:T(1,128)}) %all-reduce.40.cloned.1.call-update) | async-done | bytes 3932176
  1301.2 82.6 %reduce-scatter.19.cloned.1.call-done = f32[1,64,640]{2,1,0:T(8,128)} async-done(((f32[1,1024,640]{2,1,0:T(8,128)}), f32[1,64,640]{2,1,0:T(8,128)}) %reduce-scatter.19.cloned.1.call-update) | async-done | bytes 163856 | tf_op jit(solution)/shard_map/reduce_scatter | solution.py:313
  1383.8 117.2 %reduce-scatter.23.cloned.1.call-done = f32[1,128,640]{2,1,0:T(8,128)} async-done(((f32[1,2048,640]{2,1,0:T(8,128)}), f32[1,128,640]{2,1,0:T(8,128)}) %reduce-scatter.23.cloned.1.call-update) | async-done | bytes 327696 | tf_op jit(solution)/shard_map/reduce_scatter | solution.py:315
  1501.0 221.7 %reduce-scatter.21.cloned.1.call-done = f32[1,640,256]{2,1,0:T(8,128)} async-done(((f32[1,640,4096]{2,1,0:T(8,128)}), f32[1,640,256]{2,1,0:T(8,128)}) %reduce-scatter.21.cloned.1.call-update) | async-done | bytes 655376 | tf_op jit(solution)/shard_map/reduce_scatter | solution.py:314
  (1137 shorter events, 254.8 us)
Async XLA Ops:
  7.2 66.7 %all-gather.13.cloned.1.call-start = ((), (), s32[]{:S(2)}) async-start(), calls=%async_computation.8 | async-start | bytes 2088960 | tf_op jit(solution)/shard_map/all_gather | solution.py:253
  7.9 108.6 %all-gather.15.cloned.1.call-start = ((), (), s32[]{:S(2)}) async-start(), calls=%async_computation.9 | async-start | bytes 1179648 | tf_op jit(solution)/shard_map/all_gather | solution.py:148
  55.1 22.4 %copy-start.251 = (f32[128]{0:T(128)}, f32[128]{0:T(128)S(1)}, u32[]{:S(2)}) copy-start(f32[128]{0:T(128)S(1)} %multiply_power_fusion) | copy-start | bytes 1540
  56.2 21.3 %copy-start.296 = (f32[128]{0:T(128)}, f32[128]{0:T(128)S(1)}, u32[]{:S(2)}) copy-start(f32[128]{0:T(128)S(1)} %add_rsqrt_fusion.23) | copy-start | bytes 1540
  57.5 23.3 %copy-start.245 = (f32[1,256]{1,0:T(1,128)}, f32[1,256]{1,0:T(1,128)S(1)}, u32[]{:S(2)}) copy-start(f32[1,256]{1,0:T(1,128)S(1)} %get-tuple-element.228) | copy-start | bytes 3076
  57.5 289.2 %copy-start.241 = (f32[1,256]{1,0:T(1,128)}, f32[1,256]{1,0:T(1,128)S(1)}, u32[]{:S(2)}) copy-start(f32[1,256]{1,0:T(1,128)S(1)} %get-tuple-element.227) | copy-start | bytes 3076
  77.6 97.4 %all-gather.17.cloned.1.call-start = ((), (), s32[]{:S(2)}) async-start(), calls=%async_computation.10 | async-start | bytes 1392640 | tf_op jit(solution)/shard_map/all_gather | solution.py:254
  78.3 197.5 %all-gather.19.cloned.1.call-start = ((), (), s32[]{:S(2)}) async-start(), calls=%async_computation.11 | async-start | bytes 5570560 | tf_op jit(solution)/shard_map/all_gather | solution.py:255
  78.9 261.7 %all-gather.21.cloned.1.call-start = ((), (), s32[]{:S(2)}) async-start(), calls=%async_computation.12 | async-start | bytes 2785280 | tf_op jit(solution)/shard_map/all_gather | solution.py:256
  79.5 308.7 %all-gather.23.cloned.1.call-start = ((), (), s32[]{:S(2)}) async-start(), calls=%async_computation.13 | async-start | bytes 1179648 | tf_op jit(solution)/shard_map/all_gather | solution.py:148
  80.1 264.4 %copy-start.288 = (s32[128]{0:T(128)}, s32[128]{0:T(128)S(1)}, u32[]{:S(2)}) copy-start(s32[128]{0:T(128)S(1)} %get-tuple-element.101) | copy-start | bytes 1540
  80.1 264.4 %copy-start.289 = (s32[128]{0:T(128)}, s32[128]{0:T(128)S(1)}, u32[]{:S(2)}) copy-start(s32[128]{0:T(128)S(1)} %get-tuple-element.241) | copy-start | bytes 1540
  80.2 39.4 %copy-start.247 = (s32[512]{0:T(512)}, s32[512]{0:T(512)S(1)}, u32[]{:S(2)}) copy-start(s32[512]{0:T(512)S(1)} %get-tuple-element.300) | copy-start | bytes 6148
  81.3 37.2 %copy-start.232 = (bf16[4,128,256]{2,1,0:T(8,128)(2,1)}, bf16[4,128,256]{2,1,0:T(8,128)(2,1)S(1)}, u32[]{:S(2)}) copy-start(bf16[4,128,256]{2,1,0:T(8,128)(2,1)S(1)} %copy.153) | copy-start | bytes 786436
  121.5 154.3 %copy-start.238 = (bf16[512,256]{1,0:T(8,128)(2,1)}, bf16[512,256]{1,0:T(8,128)(2,1)S(1)}, u32[]{:S(2)}) copy-start(bf16[512,256]{1,0:T(8,128)(2,1)S(1)} %get-tuple-element.264) | copy-start | bytes 786436
  121.5 55.3 %copy-start.15 = (bf16[1,3,1,128,640]{4,3,2,1,0:T(8,128)(2,1)S(1)}, bf16[1,3,1,128,640]{4,3,2,1,0:T(8,128)(2,1)}, u32[]{:S(2)}) copy-start(bf16[1,3,1,128,640]{4,3,2,1,0:T(8,128)(2,1)} %param.7) | copy-start | bytes 1474564
  177.8 97.9 %copy-start.79 = (bf16[128,640]{1,0:T(8,128)(2,1)}, bf16[128,640]{1,0:T(8,128)(2,1)S(1)}, u32[]{:S(2)}) copy-start(bf16[128,640]{1,0:T(8,128)(2,1)S(1)} %multiply_convert_fusion.7) | copy-start | bytes 491524
  280.9 62.2 %copy-start.34 = (bf16[128,2048]{1,0:T(8,128)(2,1)}, bf16[128,2048]{1,0:T(8,128)(2,1)S(1)}, u32[]{:S(2)}) copy-start(bf16[128,2048]{1,0:T(8,128)(2,1)S(1)} %fusion.150) | copy-start | bytes 1572868
  280.9 64.7 %copy-start.8 = (bf16[1,640,1536]{1,2,0:T(8,128)(2,1)S(1)}, bf16[1,640,1536]{1,2,0:T(8,128)(2,1)}, u32[]{:S(2)}) copy-start(bf16[1,640,1536]{1,2,0:T(8,128)(2,1)} %all-gather.13.cloned.1.call-done) | copy-start | bytes 5898244
  343.2 2.3 collective-permute-start
  345.6 51.6 %copy-start.21 = (bf16[128,640]{1,0:T(8,128)(2,1)}, bf16[128,640]{1,0:T(8,128)(2,1)S(1)}, u32[]{:S(2)}) copy-start(bf16[128,640]{1,0:T(8,128)(2,1)S(1)} %get-tuple-element.147) | copy-start | bytes 491524
  348.4 105.4 %all-gather.27.cloned.1.call-start = ((), (), s32[]{:S(2)}) async-start(), calls=%async_computation.15 | async-start | bytes 1179648 | tf_op jit(solution)/shard_map/all_gather | solution.py:148
  353.7 36.5 %copy-start.229 = (bf16[4,128,256]{2,1,0:T(8,128)(2,1)}, bf16[4,128,256]{2,1,0:T(8,128)(2,1)S(1)}, u32[]{:S(2)}) copy-start(bf16[4,128,256]{2,1,0:T(8,128)(2,1)S(1)} %copy.157) | copy-start | bytes 786436
  407.6 2.4 collective-permute-start.1
  414.7 105.6 %all-gather.33.cloned.1.call-start = ((), (), s32[]{:S(2)}) async-start(), calls=%async_computation.20 | async-start | bytes 1179648 | tf_op jit(solution)/shard_map/all_gather | solution.py:148
  472.3 2.4 collective-permute-start.3
  481.3 80.2 %all-gather.29.cloned.1.call-start = ((), (), s32[]{:S(2)}) async-start(), calls=%async_computation.16 | async-start | bytes 1179648 | tf_op jit(solution)/shard_map/all_gather | solution.py:225
  481.3 9.3 copy-start.211
  482.0 120.4 %all-gather.25.cloned.1.call-start = ((), (), s32[]{:S(2)}) async-start(), calls=%async_computation.14 | async-start | bytes 1179648 | tf_op jit(solution)/shard_map/all_gather | solution.py:225
  484.0 188.6 %reduce-scatter.11.cloned.1.call-start = ((), (), s32[]{:S(2)}) async-start(), calls=%async_computation.17 | async-start | bytes 2359296 | tf_op jit(solution)/shard_map/reduce_scatter | solution.py:227
  488.1 32.3 %copy-start.250 = (s32[512]{0:T(512)S(1)}, s32[512]{0:T(512)}, u32[]{:S(2)}) copy-start(s32[512]{0:T(512)} %copy-done.247) | copy-start | bytes 6148
  492.5 49.3 %copy-start.328 = (f32[128]{0:T(128)}, f32[128]{0:T(128)S(1)}, u32[]{:S(2)}) copy-start(f32[128]{0:T(128)S(1)} %multiply_multiply_fusion.43) | copy-start | bytes 1540
  529.5 13.7 slice-start
  534.3 9.0 slice-start.1
  568.0 147.0 %all-gather.31.cloned.1.call-start = ((), (), s32[]{:S(2)}) async-start(), calls=%async_computation.19 | async-start | bytes 1179648 | tf_op jit(solution)/shard_map/all_gather | solution.py:225
  576.8 207.1 %reduce-scatter.13.cloned.1.call-start = ((), (), s32[]{:S(2)}) async-start(), calls=%async_computation.18 | async-start | bytes 2359296 | tf_op jit(solution)/shard_map/reduce_scatter | solution.py:227
  602.4 70.2 %copy-start.255 = (f32[128]{0:T(128)S(1)}, f32[128]{0:T(128)}, u32[]{:S(2)}) copy-start(f32[128]{0:T(128)} %copy-done.251) | copy-start | bytes 1540
  602.4 70.2 %copy-start.313 = (f32[128]{0:T(128)S(1)}, f32[128]{0:T(128)}, u32[]{:S(2)}) copy-start(f32[128]{0:T(128)} %get-tuple-element.233) | copy-start | bytes 1540
  602.4 74.1 %copy-start.246 = (f32[1,256]{1,0:T(1,128)S(1)}, f32[1,256]{1,0:T(1,128)}, u32[]{:S(2)}) copy-start(f32[1,256]{1,0:T(1,128)} %copy-done.245) | copy-start | bytes 3076
  685.8 7.9 slice-start.2
  688.0 3.4 collective-permute-start.2
  703.8 11.2 copy-start.317
  703.9 128.6 %all-gather.35.cloned.1.call-start = ((), (), s32[]{:S(2)}) async-start(), calls=%async_computation.22 | async-start | bytes 1179648 | tf_op jit(solution)/shard_map/all_gather | solution.py:225
  712.7 182.5 %reduce-scatter.15.cloned.1.call-start = ((), (), s32[]{:S(2)}) async-start(), calls=%async_computation.21 | async-start | bytes 2359296 | tf_op jit(solution)/shard_map/reduce_scatter | solution.py:227
  718.6 65.3 %copy-start.312 = (f32[128]{0:T(128)S(1)}, f32[128]{0:T(128)}, u32[]{:S(2)}) copy-start(f32[128]{0:T(128)} %get-tuple-element.122) | copy-start | bytes 1540
  793.6 9.9 copy-start.342
  797.2 7.9 slice-start.4
  799.4 3.4 collective-permute-start.4
  815.2 178.8 %reduce-scatter.17.cloned.1.call-start = ((), (), s32[]{:S(2)}) async-start(), calls=%async_computation.23 | async-start | bytes 2359296 | tf_op jit(solution)/shard_map/reduce_scatter | solution.py:227
  818.2 11.4 copy-start.330
  818.2 14.3 copy-start.316
  836.2 59.0 %copy-start.311 = (f32[128]{0:T(128)S(1)}, f32[128]{0:T(128)}, u32[]{:S(2)}) copy-start(f32[128]{0:T(128)} %get-tuple-element.239) | copy-start | bytes 1540
  903.0 9.0 copy-start.333
  904.7 11.0 copy-start.336
  908.4 8.8 slice-start.6
  910.6 3.4 collective-permute-start.5
  927.1 205.1 %reduce-scatter.25.cloned.1.call-start = ((), (), s32[]{:S(2)}) async-start(), calls=%async_computation.27 | async-start | bytes 1671168
  945.7 48.4 %copy-start.310 = (f32[128]{0:T(128)S(1)}, f32[128]{0:T(128)}, u32[]{:S(2)}) copy-start(f32[128]{0:T(128)} %get-tuple-element.99) | copy-start | bytes 1540
  945.7 51.8 %copy-start.30 = (f32[128,4,256]{2,1,0:T(4,128)S(1)}, f32[128,4,256]{2,1,0:T(4,128)}, u32[]{:S(2)}) copy-start(f32[128,4,256]{2,1,0:T(4,128)} %reshape.1915) | copy-start | bytes 1572868
  1008.5 291.0 %all-reduce.40.cloned.1.call-start = ((), (), s32[]{:S(2)}) async-start(), calls=%async_computation.28 | async-start | bytes 7864320
  1023.9 359.9 %reduce-scatter.19.cloned.1.call-start = ((), (), s32[]{:S(2)}) async-start(), calls=%async_computation.24 | async-start | bytes 2785280 | tf_op jit(solution)/shard_map/reduce_scatter | solution.py:313
  1034.6 466.3 %reduce-scatter.23.cloned.1.call-start = ((), (), s32[]{:S(2)}) async-start(), calls=%async_computation.26 | async-start | bytes 5570560 | tf_op jit(solution)/shard_map/reduce_scatter | solution.py:315
  1042.6 8.0 copy-start.66
  1042.6 680.0 %reduce-scatter.21.cloned.1.call-start = ((), (), s32[]{:S(2)}) async-start(), calls=%async_computation.25 | async-start | bytes 11141120 | tf_op jit(solution)/shard_map/reduce_scatter | solution.py:314
  (331 other events, 998.9 us)
Sparse Core Ops, SparseCore 0:
  10.8 63.0 all-gather.12
  77.7 38.7 all-gather.14
  119.3 55.6 all-gather.16
  177.6 98.1 all-gather.18
  278.3 62.1 all-gather.20
  348.6 39.5 all-gather.22
  414.9 38.9 all-gather.26
  481.4 38.9 all-gather.32
  522.5 38.9 all-gather.28
  563.5 38.8 all-gather.24
  606.0 66.5 reduce-scatter.10
  674.6 39.1 all-gather.30
  717.3 66.6 reduce-scatter.12
  785.9 39.2 all-gather.34
  828.6 66.5 reduce-scatter.14
  927.2 66.7 reduce-scatter.16
  1008.7 123.5 reduce-scatter.24
  1137.9 161.5 all-reduce.39
  1302.3 81.3 reduce-scatter.18
  1386.5 114.4 reduce-scatter.22
  1503.9 218.7 reduce-scatter.20
where the time goes:
time: 1740 us; the launch traced here: 1730 us
  waiting for transfers between devices  1270 us (73%)
  matrix products  157 us (9%)
  other arithmetic  118 us (7%)
  local copies, waits for them, and re-layouts  105 us (6%)
  blocking collectives  44.1 us (3%)
  between operations  21.2 us (1%)
    reduce_scatter x4, waiting for transfers between devices, backward_layer(): lax.psum_scatter(grad_keys, 'seq', scatter_dimension=0, tiled=True)  236 us
    unnamed x23, waiting for transfers between devices  225 us
    reduce_scatter x1, waiting for transfers between devices, on_device(): lax.psum_scatter(totals[2][None], ('dp', 'seq'), scatter_dimension=2, til...  222 us
    all_gather x4, waiting for transfers between devices, forward_layer(): lax.all_gather(packed, 'seq', axis=0, tiled=True)  126 us
    reduce_scatter x1, waiting for transfers between devices, on_device(): lax.psum_scatter(totals[3][None], ('dp', 'seq'), scatter_dimension=1, til...  117 us
    all_gather x1, waiting for transfers between devices, on_device(): lax.all_gather(w_gate_up, ('dp', 'seq'), axis=2, tiled=True)  97.9 us
    reduce_scatter x1, waiting for transfers between devices, on_device(): lax.psum_scatter(totals[1][None], ('dp', 'seq'), scatter_dimension=1, til...  82.6 us
    dot_general x24, matrix products, contract_rows(): lax.dot_general(left, right, (((0,), (0,)), ((), ())), preferred_element_...  61.4 us
  transfers between devices with their start and end apart: 27, of which 25 were waited for; matrix products, arithmetic and copies ran while one was open for 15% of the time, Pallas kernels for 0%

commit v1 on v0

v1 whole, which is shorter than its diff:
```python
import jax
import jax.numpy as jnp
from jax import lax
from jax.sharding import PartitionSpec as P

D = 640
HEADS = 4
HEAD_DIM = 256
FF = 2048
WINDOW = 512


epsilon = 1e-06
negative = -1e30


def rms_scale(values, scale_gain):
    return (
        values * lax.rsqrt(jnp.mean(values * values, axis=-1, keepdims=True) + epsilon) * scale_gain
    )


def geglu(gate_up):
    return jax.nn.gelu(gate_up[:, :FF], approximate=True) * gate_up[:, FF:]


def contract_rows(left, right):
    return lax.dot_general(
        left, right, (((0,), (0,)), ((), ())), preferred_element_type=jnp.float32
    )


def contract_cols(left, right):
    return lax.dot_general(
        left, right, (((1,), (1,)), ((), ())), preferred_element_type=jnp.float32
    )


def swapped(array):
    return lax.ppermute(array, "pipe", [(0, 1), (1, 0)])


def rotate(values, cosine, sine_part):
    half_size = values.shape[-1] // 2
    front_half = values[..., :half_size]
    back_half = values[..., half_size:]
    return jnp.concatenate(
        [front_half * cosine - back_half * sine_part, back_half * cosine + front_half * sine_part],
        axis=-1,
    )


def angle_tables(position, rope_base):
    half_size = HEAD_DIM // 2
    frequency = rope_base ** (-2.0 * jnp.arange(half_size, dtype=jnp.float32) / HEAD_DIM)
    angles = position.astype(jnp.float32)[..., None] * frequency
    return (jnp.cos(angles), jnp.sin(angles))


def stack_heads(rows, micro_count):
    return jnp.stack(
        [
            rows[:, h * HEAD_DIM : (h + 1) * HEAD_DIM].reshape(micro_count, -1, HEAD_DIM)
            for h in range(HEADS)
        ],
        axis=1,
    )


def side_by_side(stacked):
    return jnp.concatenate([stacked[:, h].reshape(-1, HEAD_DIM) for h in range(HEADS)], axis=1)


def split_heads(projected, query_gain, key_gain, tables):
    cosine, sine_part = tables
    micro_count = cosine.shape[0]
    width = HEADS * HEAD_DIM
    queries = stack_heads(projected[:, :width], micro_count)
    queries = rotate(rms_scale(queries, query_gain), cosine[:, None], sine_part[:, None])
    key_rows = projected[:, width : width + HEAD_DIM].reshape(micro_count, -1, HEAD_DIM)
    key_rows = rotate(rms_scale(key_rows, key_gain), cosine, sine_part)
    value_rows = projected[:, width + HEAD_DIM :].reshape(micro_count, -1, HEAD_DIM)
    return (queries, key_rows, value_rows)


def by_micro(equation, left, right):
    return jnp.einsum(equation, left, right, preferred_element_type=jnp.float32)


def visibility(query_index, position, key_index, window):
    distance = query_index[None, :, None] - key_index[None, None, :]
    visible = (distance >= 0) & (distance <= position[:, :, None])
    if window is not None:
        visible = visible & (distance < window)
    return visible


def gather_keys(packed):
    everyone = lax.all_gather(packed, ("pipe", "seq"), axis=0)
    micro_count = packed.shape[0]
    return everyone.transpose(1, 0, 2, 3).reshape(micro_count, -1, 2 * HEAD_DIM)


def scatter_keys(grad_keys, row_count):
    micro_count = grad_keys.shape[0]
    pieces = grad_keys.reshape(micro_count, -1, row_count, 2 * HEAD_DIM).transpose(1, 0, 2, 3)
    pieces = pieces.reshape(-1, 2 * HEAD_DIM)
    own = lax.psum_scatter(pieces, ("pipe", "seq"), scatter_dimension=0, tiled=True)
    return own.reshape(micro_count, row_count, 2 * HEAD_DIM).astype(jnp.float32)


def forward_layer(inputs, weights, tables, visible):
    w_qkv, w_out, w_gate_up, w_down, gains = weights
    micro_count, row_count = tables[0].shape[:2]
    normed = rms_scale(inputs, gains[:D]).astype(jnp.bfloat16)
    projected = contract_cols(normed, w_qkv)
    queries, key_rows, value_rows = split_heads(
        projected, gains[4 * D : 4 * D + HEAD_DIM], gains[4 * D + HEAD_DIM :], tables
    )
    packed = jnp.concatenate([key_rows, value_rows], axis=-1).astype(jnp.bfloat16)
    keys = gather_keys(packed)
    queries = queries.astype(jnp.bfloat16).reshape(micro_count, HEADS * row_count, HEAD_DIM)
    scores = by_micro("mqd,mkd->mqk", queries, keys[..., :HEAD_DIM]) * HEAD_DIM ** (-0.5)
    scores = jnp.where(visible, scores, negative)
    top_score = jnp.max(scores, axis=-1, keepdims=True)
    unscaled = jnp.where(visible, jnp.exp(scores - top_score), 0.0)
    denominator = jnp.sum(unscaled, axis=-1, keepdims=True)
    probability = unscaled / denominator
    gathered = by_micro("mqk,mkd->mqd", probability.astype(jnp.bfloat16), keys[..., HEAD_DIM:])
    attended = side_by_side(
        gathered.reshape(micro_count, HEADS, row_count, HEAD_DIM).astype(jnp.bfloat16)
    )
    branch = jnp.dot(attended, w_out, preferred_element_type=jnp.float32)
    hidden = inputs + rms_scale(branch, gains[D : 2 * D])
    normed_ffw = rms_scale(hidden, gains[2 * D : 3 * D]).astype(jnp.bfloat16)
    gate_up = contract_cols(normed_ffw, w_gate_up)
    activated = geglu(gate_up).astype(jnp.bfloat16)
    branch_ffw = jnp.dot(activated, w_down, preferred_element_type=jnp.float32)
    output = hidden + rms_scale(branch_ffw, gains[3 * D : 4 * D])
    kept = (
        inputs, normed, projected, queries, keys, probability, gathered, attended,
        branch, hidden, normed_ffw, gate_up, activated, branch_ffw,
    )
    return (output, kept)


def backward_layer(incoming, kept, weights, tables):
    w_qkv, w_out, w_gate_up, w_down, gains = weights
    (
        inputs, normed, projected, queries, keys, probability, gathered, attended,
        branch, hidden, normed_ffw, gate_up, activated, branch_ffw,
    ) = kept
    micro_count, row_count = tables[0].shape[:2]
    score_scale = HEAD_DIM ** (-0.5)
    unused, pullback = jax.vjp(rms_scale, branch_ffw, gains[3 * D : 4 * D])
    grad_branch_ffw, gain_post_ffw = pullback(incoming)
    grad_branch_ffw = grad_branch_ffw.astype(jnp.bfloat16)
    grad_w_down = contract_rows(activated, grad_branch_ffw)
    grad_activated = contract_cols(grad_branch_ffw, w_down)
    unused, pullback = jax.vjp(geglu, gate_up)
    grad_gate_up = pullback(grad_activated)[0].astype(jnp.bfloat16)
    grad_w_gate_up = contract_rows(grad_gate_up, normed_ffw)
    grad_normed_ffw = jnp.dot(grad_gate_up, w_gate_up, preferred_element_type=jnp.float32)
    unused, pullback = jax.vjp(rms_scale, hidden, gains[2 * D : 3 * D])
    grad_hidden, gain_pre_ffw = pullback(grad_normed_ffw)
    grad_hidden = grad_hidden + incoming
    unused, pullback = jax.vjp(rms_scale, branch, gains[D : 2 * D])
    grad_branch, gain_post_attn = pullback(grad_hidden)
    grad_branch = grad_branch.astype(jnp.bfloat16)
    grad_w_out = contract_rows(attended, grad_branch)
    grad_attended = contract_cols(grad_branch, w_out).astype(jnp.bfloat16)
    grad_rows = stack_heads(grad_attended, micro_count)
    grad_rows = grad_rows.reshape(micro_count, HEADS * row_count, HEAD_DIM)
    row_delta = jnp.sum(grad_rows.astype(jnp.float32) * gathered, axis=-1, keepdims=True)
    grad_probability = by_micro("mqd,mkd->mqk", grad_rows, keys[..., HEAD_DIM:])
    grad_scores = (probability * (grad_probability - row_delta)).astype(jnp.bfloat16)
    key_part = by_micro("mqk,mqd->mkd", grad_scores, queries) * score_scale
    value_part = by_micro("mqk,mqd->mkd", probability.astype(jnp.bfloat16), grad_rows)
    grad_keys = jnp.concatenate([key_part, value_part], axis=-1).astype(jnp.bfloat16)
    grad_keys = scatter_keys(grad_keys, row_count)
    grad_queries = by_micro("mqk,mkd->mqd", grad_scores, keys[..., :HEAD_DIM]) * score_scale
    grad_queries = grad_queries.reshape(micro_count, HEADS, row_count, HEAD_DIM)
    unused, pullback = jax.vjp(
        lambda projected, query_gain, key_gain: split_heads(
            projected, query_gain, key_gain, tables
        ),
        projected,
        gains[4 * D : 4 * D + HEAD_DIM],
        gains[4 * D + HEAD_DIM :],
    )
    grad_projected, gain_query, gain_key = pullback(
        (grad_queries, grad_keys[..., :HEAD_DIM], grad_keys[..., HEAD_DIM:])
    )
    grad_projected = grad_projected.astype(jnp.bfloat16)
    grad_w_qkv = contract_rows(grad_projected, normed)
    grad_normed = jnp.dot(grad_projected, w_qkv, preferred_element_type=jnp.float32)
    unused, pullback = jax.vjp(rms_scale, inputs, gains[:D])
    grad_inputs, gain_pre_attn = pullback(grad_normed)
    grad_inputs = grad_inputs + grad_hidden
    gain_grads = jnp.concatenate(
        [gain_pre_attn, gain_post_attn, gain_pre_ffw, gain_post_ffw, gain_query, gain_key]
    )
    return (grad_inputs, (grad_w_qkv, grad_w_out, grad_w_gate_up, grad_w_down, gain_grads))


def both_layers(shard, leading):
    own = lax.all_gather(shard, ("dp", "seq"), axis=0)
    other = swapped(own)
    return (own, other)


def rows_of(pair, layer, leading, begin, count):
    own, other = pair
    first = leading if layer == 0 else jnp.logical_not(leading)
    piece = jnp.where(first, own[:, begin : begin + count], other[:, begin : begin + count])
    return piece.reshape(-1, piece.shape[-1])


def reduce_group(grads, leading, owners):
    pieces = jnp.concatenate(
        [g.astype(jnp.bfloat16).reshape(owners, -1, D) for g in grads], axis=1
    )
    half = pieces.shape[1] // 2
    front, back = pieces[:, :half], pieces[:, half:]
    received = swapped(jnp.where(leading, back, front))
    summed = jnp.where(leading, front, back) + received
    summed = summed.reshape(owners * half, D)
    return lax.psum_scatter(summed, ("dp", "seq"), scatter_dimension=0, tiled=True)


def hand_over(lower, upper, leading):
    sent = jnp.where(leading, upper, lower)
    mine = jnp.where(leading, lower, upper)
    received = swapped(sent)
    return (jnp.where(leading, mine, received), jnp.where(leading, received, mine))


GAIN_ROWS = 16


def on_device(section_feeds, positions, w_qkv, w_out, w_gate_up, w_down, gains):
    leading = lax.axis_index("pipe") == 0
    pipe_rank = lax.axis_index("pipe")
    seq_rank = lax.axis_index("seq")
    seq_size = lax.axis_size("seq")
    owners = lax.axis_size("dp") * seq_size
    qkv_rows, out_rows = w_qkv.shape[2], w_out.shape[1]
    gate_up_rows, down_rows = w_gate_up.shape[2], w_down.shape[1]
    gain_count = gains.shape[1]
    gain_block = jnp.pad(gains, ((0, GAIN_ROWS - 1), (0, D - gain_count)))
    early = jnp.concatenate([w_qkv[0].T, w_out[0], gain_block], axis=0)
    late = jnp.concatenate([w_gate_up[0].T, w_down[0]], axis=0)
    early = both_layers(early, leading)
    late = both_layers(late, leading)

    def layer_weights(layer):
        own_gains = rows_of(early, layer, leading, qkv_rows + out_rows, 1)
        return (
            rows_of(early, layer, leading, 0, qkv_rows),
            rows_of(early, layer, leading, qkv_rows, out_rows),
            rows_of(late, layer, leading, 0, gate_up_rows),
            rows_of(late, layer, leading, gate_up_rows, down_rows),
            own_gains[:, :gain_count].reshape(-1).astype(jnp.float32),
        )

    feeds = section_feeds[0, :, 0]
    micro_count, shard_rows = feeds.shape[:2]
    row_count = shard_rows // 2
    front, back = feeds[:, :row_count], feeds[:, row_count:]
    received = swapped(jnp.where(leading, back, front))
    first_in = jnp.where(leading, front, received).reshape(-1, D)
    last_grad = jnp.where(leading, received, back).reshape(-1, D)
    begin = pipe_rank * row_count
    position = lax.dynamic_slice_in_dim(positions[:, 0], begin, row_count, 1)
    local_rows = jnp.arange(row_count, dtype=jnp.int32)
    query_index = seq_rank * shard_rows + begin + local_rows
    key_index = (
        jnp.arange(2, dtype=jnp.int32)[:, None, None] * row_count
        + jnp.arange(seq_size, dtype=jnp.int32)[None, :, None] * shard_rows
        + local_rows[None, None, :]
    ).reshape(-1)
    query_index = jnp.tile(query_index, HEADS)
    query_place = jnp.tile(position, (1, HEADS))

    lower = layer_weights(0)
    upper = layer_weights(1)
    tables = (angle_tables(position, 1000000.0), angle_tables(position, 10000.0))
    visible = (
        visibility(query_index, query_place, key_index, None),
        visibility(query_index, query_place, key_index, WINDOW),
    )
    middle, kept_lower = forward_layer(first_in.astype(jnp.float32), lower, tables[0], visible[0])
    middle = middle.astype(jnp.bfloat16).astype(jnp.float32)
    output, kept_upper = forward_layer(middle, upper, tables[1], visible[1])
    output = output.astype(jnp.bfloat16)

    def reduce_layer(grads):
        grad_qkv, grad_out, grad_gate_up, grad_down, gain_grads = grads
        gain_rows = jnp.pad(
            gain_grads.reshape(owners, 1, gain_count),
            ((0, 0), (0, GAIN_ROWS - 1), (0, D - gain_count)),
        )
        return (
            reduce_group((grad_gate_up, grad_down), leading, owners),
            reduce_group((grad_qkv, grad_out, gain_rows), leading, owners),
        )

    grad_middle, grads = backward_layer(last_grad.astype(jnp.float32), kept_upper, upper, tables[1])
    upper_parts = reduce_layer(grads)
    grad_middle = grad_middle.astype(jnp.bfloat16).astype(jnp.float32)
    grad_input, grads = backward_layer(grad_middle, kept_lower, lower, tables[0])
    lower_parts = reduce_layer(grads)
    ends = hand_over(
        grad_input.astype(jnp.bfloat16).reshape(micro_count, row_count, D),
        output.reshape(micro_count, row_count, D),
        leading,
    )
    section_end = jnp.concatenate(ends, axis=1)
    late_grads = jnp.concatenate(hand_over(lower_parts[0], upper_parts[0], leading), axis=0)
    early_grads = jnp.concatenate(hand_over(lower_parts[1], upper_parts[1], leading), axis=0)
    late_grads = late_grads.astype(jnp.float32)
    early_grads = early_grads.astype(jnp.float32)
    return (
        section_end[None, :, None],
        early_grads[:qkv_rows].T[None],
        early_grads[qkv_rows : qkv_rows + out_rows][None],
        late_grads[:gate_up_rows].T[None],
        late_grads[gate_up_rows:][None],
        early_grads[qkv_rows + out_rows, :gain_count][None],
    )


def solution(mesh):
    in_specs = (
        P("pipe", None, "dp", "seq", None),
        P(None, "dp", "seq"),
        P("pipe", None, ("dp", "seq")),
        P("pipe", ("dp", "seq"), None),
        P("pipe", None, ("dp", "seq")),
        P("pipe", ("dp", "seq"), None),
        P("pipe", ("dp", "seq")),
    )
    out_specs = (
        P("pipe", None, "dp", "seq", None),
        P("pipe", None, ("dp", "seq")),
        P("pipe", ("dp", "seq"), None),
        P("pipe", None, ("dp", "seq")),
        P("pipe", ("dp", "seq"), None),
        P("pipe", ("dp", "seq")),
    )
    return jax.shard_map(
        on_device, mesh=mesh, in_specs=in_specs, out_specs=out_specs, check_vma=False
    )
```

time: 1740 us -> 983 us (0.56)
  waiting for transfers between devices: 1270 us -> 753 us
  matrix products: 157 us -> 64.2 us
  other arithmetic: 118 us -> 70 us
  blocking collectives: 44.1 us -> 0 us
  local copies, waits for them, and re-layouts: 105 us -> 68.4 us
    reduce_scatter x7 -> x4, waiting for transfers between devices: 657 us -> 383 us  [the longest x2 273 us: reduce_group(): lax.psum_scatter(summed, ('dp', 'seq'), scatter_dimension=0, tiled=True)]
    all_gather x12 -> x4, waiting for transfers between devices: 383 us -> 233 us  [the longest x2 169 us: both_layers(): own = lax.all_gather(shard, ('dp', 'seq'), axis=0)]
    unnamed x23 -> x12, waiting for transfers between devices: 225 us -> 118 us
    dot_general x24 -> x8, matrix products: 61.4 us -> 13.3 us  [contract_rows(): lax.dot_general(left, right, (((0,), (0,)), ((), ())), preferred_element_...]
    unnamed x1 -> x0, blocking collectives: 44.1 us -> none
    dot_general x28 -> x8, matrix products: 47.9 us -> 11.6 us  [contract_cols(): lax.dot_general(left, right, (((1,), (1,)), ((), ())), preferred_element_...]
    select_n x5 -> x18, other arithmetic: 3.15 us -> 28.3 us  [the longest x5 19.3 us: rows_of(): jnp.where(first, own[:, begin:begin + count], other[:, begin:begin + count])]
    reduce_sum x29 -> x6, other arithmetic: 26.1 us -> 1.16 us  [rms_scale(): jnp.mean(values * values, axis=-1, keepdims=True) + epsilon]
  transfers between devices with their start and end apart: 27 -> 20, of which waited for: 25 -> 16; matrix products, arithmetic and copies ran while one was open for 15% -> 11% of each run, Pallas kernels for 0% -> 0%
where the time goes in v1:
time: 983 us; the launch traced here: 975 us
  waiting for transfers between devices  753 us (77%)
  other arithmetic  70 us (7%)
  local copies, waits for them, and re-layouts  68.4 us (7%)
  matrix products  64.2 us (7%)
  between operations  16.6 us (2%)
    reduce_scatter x2, waiting for transfers between devices, reduce_group(): lax.psum_scatter(summed, ('dp', 'seq'), scatter_dimension=0, tiled=True)  273 us
    all_gather x2, waiting for transfers between devices, both_layers(): own = lax.all_gather(shard, ('dp', 'seq'), axis=0)  169 us
    unnamed x12, waiting for transfers between devices  118 us
    reduce_scatter x2, waiting for transfers between devices, scatter_keys(): lax.psum_scatter(pieces, ('pipe', 'seq'), scatter_dimension=0, tiled=True)  110 us
    all_gather x2, waiting for transfers between devices, gather_keys(): everyone = lax.all_gather(packed, ('pipe', 'seq'), axis=0)  63.5 us
    unnamed x319, local copies, waits for them, and re-layouts  48.1 us
  transfers between devices with their start and end apart: 20, of which 16 were waited for; matrix products, arithmetic and copies ran while one was open for 11% of the time, Pallas kernels for 0%

profile of v1, /device:TPU:0, one launch (start us, length us, event | category | flops | bytes accessed | tf_op | source)
XLA Modules:
  0.0 974.7 jit_solution(16975116101925730652)
XLA Ops:
  7.2 1.7 fusion.95
  9.0 1.1 copy.100
  10.1 1.8 pad_maximum_fusion.8
  12.0 73.7 %all-gather.11.cloned.1.call-done = bf16[2816,640]{1,0:T(8,128)(2,1)} async-done(((bf16[176,640]{1,0:T(8,128)(2,1)}), bf16[2816,640]{1,0:T(8,128)(2,1)}) %all-gather.11.cloned.1.call-update) | async-done | bytes 3604496 | tf_op jit(solution)/shard_map/all_gather | solution.py:207
  86.4 5.6 collective-permute-done
  94.0 2.8 broadcast_select_fusion.6
  97.6 1.1 slice.599
  99.6 1.6 pad_maximum_fusion.19
  101.3 95.7 %all-gather.13.cloned.1.call-done = bf16[6144,640]{0,1:T(8,128)(2,1)} async-done(((bf16[384,640]{0,1:T(8,128)(2,1)}), bf16[6144,640]{0,1:T(8,128)(2,1)}) %all-gather.13.cloned.1.call-update) | async-done | bytes 7864336 | tf_op jit(solution)/shard_map/all_gather | solution.py:207
  197.0 8.5 copy.142
  206.6 1.2 subtract_compare_fusion
  207.8 1.1 broadcast_subtract_fusion
  210.9 3.5 broadcast_select_fusion.10
  214.4 28.8 %all-gather.7.cloned.1.call-done = bf16[16,3,64,512]{3,2,1,0:T(8,128)(2,1)} async-done(((bf16[1,3,64,512]{3,2,1,0:T(8,128)(2,1)}), bf16[16,3,64,512]{3,2,1,0:T(8,128)(2,1)}) %all-gather.7.cloned.1.call-update) | async-done | bytes 3145744 | tf_op jit(solution)/shard_map/all_gather | solution.py:99
  243.2 4.1 copy.99
  247.3 5.6 fusion.186
  252.9 4.0 fusion.187
  258.4 7.4 broadcast_select_fusion
  265.8 3.7 copy.143
  269.5 1.4 fusion.162
  272.4 1.2 copy-done.4
  273.5 4.6 broadcast_select_fusion.4
  278.2 1.1 multiply_reduce_fusion.21
  284.5 8.5 copy.145
  292.9 34.7 %all-gather.9.cloned.1.call-done = bf16[16,3,64,512]{3,2,1,0:T(8,128)(2,1)} async-done(((bf16[1,3,64,512]{3,2,1,0:T(8,128)(2,1)}), bf16[16,3,64,512]{3,2,1,0:T(8,128)(2,1)}) %all-gather.9.cloned.1.call-update) | async-done | bytes 3145744 | tf_op jit(solution)/shard_map/all_gather | solution.py:99
  327.6 4.0 copy.103
  331.6 6.2 fusion.188
  337.8 3.1 fusion.189
  342.3 1.4 fusion.163
  344.4 1.5 copy-done.58
  345.8 1.1 multiply_reduce_fusion.18
  347.4 2.9 fusion.73
  350.4 2.6 multiply_reduce_fusion.8
  359.9 1.9 copy.131
  361.8 2.5 fusion.61
  367.9 59.1 %reduce-scatter.13.cloned.1.call-done = bf16[192,512]{1,0:T(8,128)(2,1)} async-done(((bf16[3072,512]{1,0:T(8,128)(2,1)}), bf16[192,512]{1,0:T(8,128)(2,1)}) %reduce-scatter.13.cloned.1.call-update) | async-done | bytes 196624 | tf_op jit(solution)/shard_map/reduce_scatter | solution.py:108
  429.4 1.1 multiply_reduce_fusion.25
  431.7 2.5 fusion.75
  434.8 1.1 copy-done.57
  435.9 2.9 fusion.72
  438.9 2.5 multiply_reduce_fusion.10
  449.3 1.9 copy.132
  452.1 1.7 convolution_convert_fusion.8
  455.4 1.9 convolution_convert_fusion.2
  457.9 1.4 copy-done.47
  463.7 1.7 convolution_convert_fusion.9
  465.4 1.9 select_add_fusion.2
  467.4 51.0 %reduce-scatter.15.cloned.1.call-done = bf16[192,512]{1,0:T(8,128)(2,1)} async-done(((bf16[3072,512]{1,0:T(8,128)(2,1)}), bf16[192,512]{1,0:T(8,128)(2,1)}) %reduce-scatter.15.cloned.1.call-update) | async-done | bytes 196624 | tf_op jit(solution)/shard_map/reduce_scatter | solution.py:108
  521.2 1.9 fusion.165
  525.1 2.1 convolution_convert_fusion.3
  529.9 1.9 convolution_convert_fusion
  531.8 2.5 broadcast_select_fusion.2
  535.3 2.0 select_add_fusion.3
  537.4 5.1 collective-permute-done.8
  542.5 5.8 select_add_fusion
  551.0 1.9 convolution_convert_fusion.1
  552.9 1.3 broadcast_select_fusion.3
  554.4 6.6 collective-permute-done.7
  561.1 2.9 select_add_fusion.1
  566.0 1.4 collective-permute-done.3
  567.4 35.3 %reduce-scatter.23.cloned.1.call-done = bf16[88,640]{1,0:T(8,128)(2,1)} async-done(((bf16[1408,640]{1,0:T(8,128)(2,1)}), bf16[88,640]{1,0:T(8,128)(2,1)}) %reduce-scatter.23.cloned.1.call-update) | async-done | bytes 112656
  602.7 82.3 %reduce-scatter.21.cloned.1.call-done = bf16[88,640]{1,0:T(8,128)(2,1)} async-done(((bf16[1408,640]{1,0:T(8,128)(2,1)}), bf16[88,640]{1,0:T(8,128)(2,1)}) %reduce-scatter.21.cloned.1.call-update) | async-done | bytes 112656
  688.9 133.5 %reduce-scatter.19.cloned.1.call-done = bf16[192,640]{1,0:T(8,128)(2,1)} async-done(((bf16[3072,640]{1,0:T(8,128)(2,1)}), bf16[192,640]{1,0:T(8,128)(2,1)}) %reduce-scatter.19.cloned.1.call-update) | async-done | bytes 245776 | tf_op jit(solution)/shard_map/reduce_scatter | solution.py:228
  822.5 139.6 %reduce-scatter.17.cloned.1.call-done = bf16[192,640]{1,0:T(8,128)(2,1)} async-done(((bf16[3072,640]{1,0:T(8,128)(2,1)}), bf16[192,640]{1,0:T(8,128)(2,1)}) %reduce-scatter.17.cloned.1.call-update) | async-done | bytes 245776 | tf_op jit(solution)/shard_map/reduce_scatter | solution.py:228
  (510 shorter events, 69.7 us)
Async XLA Ops:
  7.2 79.1 %copy-start = (s32[3,1,128]{2,1,0:T(1,128)S(1)}, s32[3,1,128]{2,1,0:T(1,128)}, u32[]{:S(2)}) copy-start(s32[3,1,128]{2,1,0:T(1,128)} %param.8) | copy-start | bytes 4612
  7.2 78.5 %copy-start.59 = (bf16[1,3,1,128,640]{4,3,2,1,0:T(8,128)(2,1)S(1)}, bf16[1,3,1,128,640]{4,3,2,1,0:T(8,128)(2,1)}, u32[]{:S(2)}) copy-start(bf16[1,3,1,128,640]{4,3,2,1,0:T(8,128)(2,1)} %param.7) | copy-start | bytes 1474564
  7.2 78.5 %all-gather.11.cloned.1.call-start = ((), (), s32[]{:S(2)}) async-start(), calls=%async_computation.12 | async-start | bytes 3829760 | tf_op jit(solution)/shard_map/all_gather | solution.py:207
  9.0 188.1 %all-gather.13.cloned.1.call-start = ((), (), s32[]{:S(2)}) async-start(), calls=%async_computation.13 | async-start | bytes 8355840 | tf_op jit(solution)/shard_map/all_gather | solution.py:207
  11.9 231.3 %all-gather.7.cloned.1.call-start = ((), (), s32[]{:S(2)}) async-start(), calls=%async_computation.6 | async-start | bytes 3342336 | tf_op jit(solution)/shard_map/all_gather | solution.py:99
  85.7 7.1 collective-permute-start.1
  85.7 6.3 collective-permute-start
  86.4 12.8 %copy-start.126 = (f32[128]{0:T(128)}, f32[128]{0:T(128)S(1)}, u32[]{:S(2)}) copy-start(f32[128]{0:T(128)S(1)} %fusion.143) | copy-start | bytes 1540
  96.8 183.5 %copy-start.11 = (bf16[16,96,640]{2,1,0:T(8,128)(2,1)}, bf16[16,96,640]{2,1,0:T(8,128)(2,1)S(1)}, u32[]{:S(2)}) copy-start(bf16[16,96,640]{2,1,0:T(8,128)(2,1)S(1)} %get-tuple-element.70) | copy-start | bytes 5898244
  98.9 106.7 %copy-start.49 = (f32[192,256]{1,0:T(8,128)}, f32[192,256]{1,0:T(8,128)S(1)}, u32[]{:S(2)}) copy-start(f32[192,256]{1,0:T(8,128)S(1)} %get-tuple-element.88) | copy-start | bytes 589828
  98.9 110.2 %copy-start.18 = (f32[192,256]{1,0:T(8,128)}, f32[192,256]{1,0:T(8,128)S(1)}, u32[]{:S(2)}) copy-start(f32[192,256]{1,0:T(8,128)S(1)} %get-tuple-element.86) | copy-start | bytes 589828
  98.9 110.2 %copy-start.20 = (f32[192,256]{1,0:T(8,128)}, f32[192,256]{1,0:T(8,128)S(1)}, u32[]{:S(2)}) copy-start(f32[192,256]{1,0:T(8,128)S(1)} %get-tuple-element.89) | copy-start | bytes 589828
  98.9 110.2 %copy-start.22 = (f32[192,256]{1,0:T(8,128)}, f32[192,256]{1,0:T(8,128)S(1)}, u32[]{:S(2)}) copy-start(f32[192,256]{1,0:T(8,128)S(1)} %get-tuple-element.90) | copy-start | bytes 589828
  98.9 110.2 %copy-start.24 = (f32[192,256]{1,0:T(8,128)}, f32[192,256]{1,0:T(8,128)S(1)}, u32[]{:S(2)}) copy-start(f32[192,256]{1,0:T(8,128)S(1)} %get-tuple-element.91) | copy-start | bytes 589828
  99.0 110.1 %copy-start.109 = (f32[256]{0:T(256)}, f32[256]{0:T(256)S(1)}, u32[]{:S(2)}) copy-start(f32[256]{0:T(256)S(1)} %get-tuple-element.152) | copy-start | bytes 3076
  99.6 109.7 %copy-start.74 = (f32[3,64,128]{2,1,0:T(8,128)}, f32[3,64,128]{2,1,0:T(8,128)S(1)}, u32[]{:S(2)}) copy-start(f32[3,64,128]{2,1,0:T(8,128)S(1)} %get-tuple-element.161) | copy-start | bytes 294916
  101.2 226.4 %all-gather.9.cloned.1.call-start = ((), (), s32[]{:S(2)}) async-start(), calls=%async_computation.7 | async-start | bytes 3342336 | tf_op jit(solution)/shard_map/all_gather | solution.py:99
  205.6 52.9 %collective-permute-start.2 = (bf16[16,384,640]{1,0,2:T(8,128)(2,1)}, bf16[16,384,640]{1,0,2:T(8,128)(2,1)}, u32[]{:S(2)}, u32[]{:S(2)}) collective-permute-start(bf16[16,384,640]{1,0,2:T(8,128)(2,1)} %bitcast.136), channel_id=1, source_target_pairs={{0,16},{16,0},{1,17},{17,1},{2,18},{18,2},{3,19},{19,3},{4,20},{20... | collective-permute-start | bytes 23592968 | tf_op jit(solution)/shard_map/ppermute | solution.py:40
  210.9 153.7 %copy-start.111 = (f32[256]{0:T(256)}, f32[256]{0:T(256)S(1)}, u32[]{:S(2)}) copy-start(f32[256]{0:T(256)S(1)} %get-tuple-element.146) | copy-start | bytes 3076
  243.2 4.1 copy-start.63
  252.9 4.0 copy-start.146
  252.9 4.1 copy-start.15
  257.6 8.2 copy-start.36
  258.4 7.4 copy-start.116
  273.5 4.6 copy-start.52
  283.2 143.8 %reduce-scatter.13.cloned.1.call-start = ((), (), s32[]{:S(2)}) async-start(), calls=%async_computation.8 | async-start | bytes 3342336 | tf_op jit(solution)/shard_map/reduce_scatter | solution.py:108
  284.4 47.2 %copy-start.90 = (bf16[3,4,64,128]{3,2,1,0:T(8,128)(2,1)}, bf16[3,4,64,128]{3,2,1,0:T(8,128)(2,1)S(1)}, u32[]{:S(2)}) copy-start(bf16[3,4,64,128]{3,2,1,0:T(8,128)(2,1)S(1)} %copy.101) | copy-start | bytes 589828
  284.5 47.2 %copy-start.92 = (bf16[3,4,64,128]{3,2,1,0:T(8,128)(2,1)}, bf16[3,4,64,128]{3,2,1,0:T(8,128)(2,1)S(1)}, u32[]{:S(2)}) copy-start(bf16[3,4,64,128]{3,2,1,0:T(8,128)(2,1)S(1)} %copy.102) | copy-start | bytes 589828
  327.6 4.0 copy-start.85
  327.6 4.0 copy-start.86
  331.6 10.7 %slice-start.2 = ((s8[5242880]{0:T(1024)(128)(4,1)}), s8[1048576]{0:T(1024)(128)(4,1)S(1)}, s32[]{:S(2)}) async-start(s8[5242880]{0:T(1024)(128)(4,1)} %bitcast.236), calls=%async_computation.18 | async-start | bytes 2097152
  337.8 3.2 copy-start.17
  337.8 4.5 slice-start.3
  342.3 10.7 %copy-start.6 = (f32[192,640]{1,0:T(8,128)}, f32[192,640]{1,0:T(8,128)S(1)}, u32[]{:S(2)}) copy-start(f32[192,640]{1,0:T(8,128)S(1)} %get-tuple-element.61) | copy-start | bytes 1474564
  347.0 3.4 copy-start.38
  347.0 3.4 copy-start.112
  361.8 156.7 %reduce-scatter.15.cloned.1.call-start = ((), (), s32[]{:S(2)}) async-start(), calls=%async_computation.9 | async-start | bytes 3342336 | tf_op jit(solution)/shard_map/reduce_scatter | solution.py:108
  366.8 62.1 %copy-start.129 = (f32[128]{0:T(128)S(1)}, f32[128]{0:T(128)}, u32[]{:S(2)}) copy-start(f32[128]{0:T(128)} %fusion.142) | copy-start | bytes 1540
  366.9 64.7 %copy-start.12 = (bf16[16,96,640]{2,1,0:T(8,128)(2,1)S(1)}, bf16[16,96,640]{2,1,0:T(8,128)(2,1)}, u32[]{:S(2)}) copy-start(bf16[16,96,640]{2,1,0:T(8,128)(2,1)} %copy-done.11) | copy-start | bytes 5898244
  366.9 64.7 %copy-start.115 = (f32[192]{0:T(256)S(1)}, f32[192]{0:T(256)}, u32[]{:S(2)}) copy-start(f32[192]{0:T(256)} %copy-done.114) | copy-start | bytes 2308
  427.0 4.6 copy-start.82
  428.9 5.2 copy-start.89
  434.2 4.7 slice-start
  451.2 3.3 copy-start.130
  451.2 4.2 copy-start.45
  451.2 4.2 copy-start.83
  451.2 151.5 %reduce-scatter.23.cloned.1.call-start = ((), (), s32[]{:S(2)}) async-start(), calls=%async_computation.15 | async-start | bytes 1914880
  457.8 7.6 collective-permute-start.5
  467.3 53.0 %copy-start.127 = (f32[128]{0:T(128)S(1)}, f32[128]{0:T(128)}, u32[]{:S(2)}) copy-start(f32[128]{0:T(128)} %copy-done.126) | copy-start | bytes 1540
  467.3 53.5 %copy-start.50 = (f32[192,256]{1,0:T(8,128)S(1)}, f32[192,256]{1,0:T(8,128)}, u32[]{:S(2)}) copy-start(f32[192,256]{1,0:T(8,128)} %copy-done.49) | copy-start | bytes 589828
  467.4 53.8 %copy-start.10 = (bf16[16,96,640]{2,1,0:T(8,128)(2,1)S(1)}, bf16[16,96,640]{2,1,0:T(8,128)(2,1)}, u32[]{:S(2)}) copy-start(bf16[16,96,640]{2,1,0:T(8,128)(2,1)} %copy-done.9) | copy-start | bytes 5898244
  467.4 217.6 %reduce-scatter.21.cloned.1.call-start = ((), (), s32[]{:S(2)}) async-start(), calls=%async_computation.14 | async-start | bytes 1914880
  523.1 4.2 copy-start.61
  523.2 4.0 copy-start.13
  527.8 7.6 collective-permute-start.4
  531.8 3.5 copy-start.2
  531.8 3.5 copy-start.14
  535.3 7.1 collective-permute-start.8
  537.4 285.1 %reduce-scatter.19.cloned.1.call-start = ((), (), s32[]{:S(2)}) async-start(), calls=%async_computation.11 | async-start | bytes 4177920 | tf_op jit(solution)/shard_map/reduce_scatter | solution.py:228
  548.3 413.8 %reduce-scatter.17.cloned.1.call-start = ((), (), s32[]{:S(2)}) async-start(), calls=%async_computation.10 | async-start | bytes 4177920 | tf_op jit(solution)/shard_map/reduce_scatter | solution.py:228
  554.2 6.8 collective-permute-start.7
  565.8 1.6 collective-permute-start.3
  685.9 1.4 collective-permute-start.6
  963.1 1.6 collective-permute-start.9
  (108 other events, 184.8 us)
Sparse Core Ops, SparseCore 0:
  11.3 74.2 all-gather.10
  89.0 108.0 all-gather.12
  199.8 43.3 all-gather.6
  283.3 44.2 all-gather.8
  361.9 65.0 reduce-scatter.12
  451.3 67.1 reduce-scatter.14
  520.8 81.8 reduce-scatter.22
  605.0 79.8 reduce-scatter.20
  690.1 132.3 reduce-scatter.18
  827.4 134.6 reduce-scatter.16

commit v2 on v1

--- a/solution.py
+++ b/solution.py
@@ -144,13 +144,14 @@
     return (output, kept)
 
 
-def backward_layer(incoming, kept, weights, tables):
+def backward_layer(incoming, kept, weights, tables, leading, pending):
     w_qkv, w_out, w_gate_up, w_down, gains = weights
     (
         inputs, normed, projected, queries, keys, probability, gathered, attended,
         branch, hidden, normed_ffw, gate_up, activated, branch_ffw,
     ) = kept
     micro_count, row_count = tables[0].shape[:2]
+    owners = lax.axis_size("dp") * lax.axis_size("seq")
     score_scale = HEAD_DIM ** (-0.5)
     unused, pullback = jax.vjp(rms_scale, branch_ffw, gains[3 * D : 4 * D])
     grad_branch_ffw, gain_post_ffw = pullback(incoming)
@@ -164,6 +165,9 @@
     unused, pullback = jax.vjp(rms_scale, hidden, gains[2 * D : 3 * D])
     grad_hidden, gain_pre_ffw = pullback(grad_normed_ffw)
     grad_hidden = grad_hidden + incoming
+    own_chains = start_group((grad_w_gate_up, grad_w_down), leading, owners)
+    if pending:
+        grad_hidden, pending = held_until(grad_hidden, advance(pending, 2))
     unused, pullback = jax.vjp(rms_scale, branch, gains[D : 2 * D])
     grad_branch, gain_post_attn = pullback(grad_hidden)
     grad_branch = grad_branch.astype(jnp.bfloat16)
@@ -178,6 +182,9 @@
     value_part = by_micro("mqk,mqd->mkd", probability.astype(jnp.bfloat16), grad_rows)
     grad_keys = jnp.concatenate([key_part, value_part], axis=-1).astype(jnp.bfloat16)
     grad_keys = scatter_keys(grad_keys, row_count)
+    waiting = advance(own_chains, 2) + advance(pending, seq_bits() + 1)
+    grad_keys, waiting = held_until(grad_keys, waiting)
+    own_chains, pending = waiting[:2], waiting[2:]
     grad_queries = by_micro("mqk,mkd->mqd", grad_scores, keys[..., :HEAD_DIM]) * score_scale
     grad_queries = grad_queries.reshape(micro_count, HEADS, row_count, HEAD_DIM)
     unused, pullback = jax.vjp(
@@ -200,12 +207,97 @@
     gain_grads = jnp.concatenate(
         [gain_pre_attn, gain_post_attn, gain_pre_ffw, gain_post_ffw, gain_query, gain_key]
     )
-    return (grad_inputs, (grad_w_qkv, grad_w_out, grad_w_gate_up, grad_w_down, gain_grads))
-
-
-def both_layers(shard, leading):
+    gain_rows = gain_grads.reshape(owners, 1, -1)
+    gain_rows = jnp.pad(gain_rows, ((0, 0), (0, GAIN_ROWS - 1), (0, D - gain_rows.shape[-1])))
+    last_chains = start_group((grad_w_qkv, grad_w_out, gain_rows), leading, owners)
+    return (grad_inputs, own_chains + last_chains, pending)
+
+
+def seq_bits():
+    return lax.axis_size("seq").bit_length() - 1
+
+
+def across(array, dim):
+    if dim == 0:
+        return lax.ppermute(array, "dp", [(0, 1), (1, 0)])
+    step = 1 << (seq_bits() - dim)
+    size = lax.axis_size("seq")
+    return lax.ppermute(array, "seq", [(i, i ^ step) for i in range(size)])
+
+
+def upper_side(dim):
+    if dim == 0:
+        return lax.axis_index("dp") == 1
+    return ((lax.axis_index("seq") >> (seq_bits() - dim)) & 1) == 1
+
+
+def halving_order(first):
+    last = seq_bits()
+    inner = list(range(last - 1, 0, -1))
+    return ([last, 0] if first else [0, last]) + inner
+
+
+def gathered_by_doubling(shard, first):
+    piece = shard.reshape((1,) * (seq_bits() + 1) + shard.shape)
+    for dim in halving_order(first)[::-1]:
+        received = across(piece, dim)
+        piece = jnp.where(
+            upper_side(dim),
+            jnp.concatenate([received, piece], axis=dim),
+            jnp.concatenate([piece, received], axis=dim),
+        )
+    return piece.reshape((-1,) + shard.shape)
+
+
+def advance(chains, count):
+    moved = []
+    for total, order in chains:
+        for dim in order[:count]:
+            low_half = lax.slice_in_dim(total, 0, 1, axis=dim)
+            high_half = lax.slice_in_dim(total, 1, 2, axis=dim)
+            high = upper_side(dim)
+            received = across(jnp.where(high, low_half, high_half), dim)
+            total = jnp.where(high, high_half, low_half) + received
+        moved.append((total, order[count:]))
+    return moved
+
+
+def finish(chains):
+    ends = [total for total, order in advance(chains, seq_bits() + 1)]
+    return jnp.concatenate([total.reshape(total.shape[-2:]) for total in ends], axis=0)
+
+
+def held_until(array, chains):
+    tied = lax.optimization_barrier((array,) + tuple(total for total, order in chains))
+    return (tied[0], [(total, chain[1]) for total, chain in zip(tied[1:], chains)])
+
+
+def start_group(grads, leading, owners):
+    pieces = jnp.concatenate(
+        [g.astype(jnp.bfloat16).reshape(owners, -1, D) for g in grads], axis=1
+    )
+    half = pieces.shape[1] // 2
+    front, back = pieces[:, :half], pieces[:, half:]
+    received = swapped(jnp.where(leading, back, front))
+    summed = jnp.where(leading, front, back) + received
+    cut = -(-half // 32) * 16 if half > 32 else half // 2
+    sizes = (2,) * (seq_bits() + 1)
+    return [
+        (piece.reshape(sizes + piece.shape[1:]), halving_order(first))
+        for piece, first in ((summed[:, :cut], True), (summed[:, cut:], False))
+    ]
+
+
+def both_layers(shard):
     own = lax.all_gather(shard, ("dp", "seq"), axis=0)
-    other = swapped(own)
+    return (own, swapped(own))
+
+
+def both_layers_by_doubling(shard):
+    half = shard.shape[0] // 2
+    chains = [gathered_by_doubling(shard[:half], True), gathered_by_doubling(shard[half:], False)]
+    own = jnp.concatenate(chains, axis=1)
+    other = jnp.concatenate([swapped(chain) for chain in chains], axis=1)
     return (own, other)
 
 
@@ -214,18 +306,6 @@
     first = leading if layer == 0 else jnp.logical_not(leading)
     piece = jnp.where(first, own[:, begin : begin + count], other[:, begin : begin + count])
     return piece.reshape(-1, piece.shape[-1])
-
-
-def reduce_group(grads, leading, owners):
-    pieces = jnp.concatenate(
-        [g.astype(jnp.bfloat16).reshape(owners, -1, D) for g in grads], axis=1
-    )
-    half = pieces.shape[1] // 2
-    front, back = pieces[:, :half], pieces[:, half:]
-    received = swapped(jnp.where(leading, back, front))
-    summed = jnp.where(leading, front, back) + received
-    summed = summed.reshape(owners * half, D)
-    return lax.psum_scatter(summed, ("dp", "seq"), scatter_dimension=0, tiled=True)
 
 
 def hand_over(lower, upper, leading):
@@ -250,8 +330,8 @@
     gain_block = jnp.pad(gains, ((0, GAIN_ROWS - 1), (0, D - gain_count)))
     early = jnp.concatenate([w_qkv[0].T, w_out[0], gain_block], axis=0)
     late = jnp.concatenate([w_gate_up[0].T, w_down[0]], axis=0)
-    early = both_layers(early, leading)
-    late = both_layers(late, leading)
+    early = both_layers(early)
+    late = both_layers_by_doubling(late)
 
     def layer_weights(layer):
         own_gains = rows_of(early, layer, leading, qkv_rows + out_rows, 1)
@@ -294,22 +374,15 @@
     output, kept_upper = forward_layer(middle, upper, tables[1], visible[1])
     output = output.astype(jnp.bfloat16)
 
-    def reduce_layer(grads):
-        grad_qkv, grad_out, grad_gate_up, grad_down, gain_grads = grads
-        gain_rows = jnp.pad(
-            gain_grads.reshape(owners, 1, gain_count),
-            ((0, 0), (0, GAIN_ROWS - 1), (0, D - gain_count)),
-        )
-        return (
-            reduce_group((grad_gate_up, grad_down), leading, owners),
-            reduce_group((grad_qkv, grad_out, gain_rows), leading, owners),
-        )
-
-    grad_middle, grads = backward_layer(last_grad.astype(jnp.float32), kept_upper, upper, tables[1])
-    upper_parts = reduce_layer(grads)
+    grad_middle, upper_chains, unused = backward_layer(
+        last_grad.astype(jnp.float32), kept_upper, upper, tables[1], leading, []
+    )
     grad_middle = grad_middle.astype(jnp.bfloat16).astype(jnp.float32)
-    grad_input, grads = backward_layer(grad_middle, kept_lower, lower, tables[0])
-    lower_parts = reduce_layer(grads)
+    grad_input, lower_chains, upper_chains = backward_layer(
+        grad_middle, kept_lower, lower, tables[0], leading, upper_chains
+    )
+    upper_parts = (finish(upper_chains[:2]), finish(upper_chains[2:]))
+    lower_parts = (finish(lower_chains[:2]), finish(lower_chains[2:]))
     ends = hand_over(
         grad_input.astype(jnp.bfloat16).reshape(micro_count, row_count, D),
         output.reshape(micro_count, row_count, D),

time: 983 us -> 642 us (0.65)
  waiting for transfers between devices: 753 us -> 366 us
  starting transfers between devices: 2.21 us -> 46 us
  other arithmetic: 70 us -> 99.9 us
  local copies, waits for them, and re-layouts: 68.4 us -> 42.7 us
    reduce_scatter x2 -> x0, waiting for transfers between devices: 273 us -> none  [reduce_group(): lax.psum_scatter(summed, ('dp', 'seq'), scatter_dimension=0, tiled=True)]
    ppermute x0 -> x40, waiting for transfers between devices: none -> 212 us  [the longest x30 134 us: across(): return lax.ppermute(array, 'seq', [(i, i ^ step) for i in range(size)])]
    all_gather x2 -> x1, waiting for transfers between devices: 169 us -> 45.7 us  [both_layers(): own = lax.all_gather(shard, ('dp', 'seq'), axis=0)]
    unnamed x12 -> x5, waiting for transfers between devices: 118 us -> 0.08 us
    reduce_scatter x2, waiting for transfers between devices: 110 us -> 39.7 us  [scatter_keys(): lax.psum_scatter(pieces, ('pipe', 'seq'), scatter_dimension=0, tiled=True)]
    ppermute x0 -> x40, starting transfers between devices: none -> 44.3 us  [the longest x30 31.1 us: across(): return lax.ppermute(array, 'seq', [(i, i ^ step) for i in range(size)])]
    unnamed x319 -> x365, local copies, waits for them, and re-layouts: 48.1 us -> 20.6 us
    select_n x4 -> x44, other arithmetic: 4.7 us -> 28.8 us  [the longest x8 16 us: gathered_by_doubling(): jnp.where(upper_side(dim), jnp.concatenate([received, piece], axis=dim),...]
  transfers between devices with their start and end apart: 20 -> 56, of which waited for: 16 -> 31; matrix products, arithmetic and copies ran while one was open for 11% -> 19% of each run, Pallas kernels for 0% -> 0%
where the time goes in v2:
time: 642 us; the launch traced here: 636 us
  waiting for transfers between devices  366 us (57%)
  other arithmetic  99.9 us (16%)
  matrix products  64.1 us (10%)
  starting transfers between devices  46 us (7%)
  local copies, waits for them, and re-layouts  42.7 us (7%)
  between operations  17.2 us (3%)
    ppermute x30, waiting for transfers between devices, across(): return lax.ppermute(array, 'seq', [(i, i ^ step) for i in range(size)])  134 us
    ppermute x10, waiting for transfers between devices, across(): return lax.ppermute(array, 'dp', [(0, 1), (1, 0)])  77.6 us
    all_gather x2, waiting for transfers between devices, gather_keys(): everyone = lax.all_gather(packed, ('pipe', 'seq'), axis=0)  67 us
    all_gather x1, waiting for transfers between devices, both_layers(): own = lax.all_gather(shard, ('dp', 'seq'), axis=0)  45.7 us
    reduce_scatter x2, waiting for transfers between devices, scatter_keys(): lax.psum_scatter(pieces, ('pipe', 'seq'), scatter_dimension=0, tiled=True)  39.7 us
    ppermute x30, starting transfers between devices, across(): return lax.ppermute(array, 'seq', [(i, i ^ step) for i in range(size)])  31.1 us
    select_n x5, other arithmetic, rows_of(): jnp.where(first, own[:, begin:begin + count], other[:, begin:begin + count])  22 us
    unnamed x365, local copies, waits for them, and re-layouts  20.6 us
  transfers between devices with their start and end apart: 56, of which 31 were waited for; matrix products, arithmetic and copies ran while one was open for 19% of the time, Pallas kernels for 0%

profile of v2, /device:TPU:0, one launch (start us, length us, event | category | flops | bytes accessed | tf_op | source)
XLA Modules:
  0.0 636.3 jit_solution(4316815225733481384)
XLA Ops:
  11.2 4.1 collective-permute-start.6
  15.3 21.7 %collective-permute-done.6 = bf16[1,1,1,1,192,640]{5,4,1,2,3,0:T(8,128)(2,1)S(1)} collective-permute-done((bf16[1,1,1,1,192,640]{5,4,1,2,3,0:T(8,128)(2,1)S(1)}, bf16[1,1,1,1,192,640]{5,4,1,2,3,0:T(8,128)(2,1)S(1)}, u32[]{:S(2)}, u32[]{:S(2)}) %collective-permute-start.6) | collective-permute-done | bytes 245792 | tf_op jit(solution)/shard_map/ppermute | solution.py:225
  37.2 4.7 collective-permute-done.2
  43.6 14.6 %collective-permute-done.7 = bf16[1,2,1,1,192,640]{5,4,1,2,3,0:T(8,128)(2,1)S(1)} collective-permute-done((bf16[1,2,1,1,192,640]{5,4,1,2,3,0:T(8,128)(2,1)S(1)}, bf16[1,2,1,1,192,640]{5,4,1,2,3,0:T(8,128)(2,1)S(1)}, u32[]{:S(2)}, u32[]{:S(2)}) %collective-permute-start.7) | collective-permute-done | bytes 491552 | tf_op jit(solution)/shard_map/ppermute | solution.py:225
  61.0 45.7 %all-gather.9.cloned.1.call-done = bf16[2816,640]{1,0:T(8,128)(2,1)} async-done(((bf16[176,640]{1,0:T(8,128)(2,1)}), bf16[2816,640]{1,0:T(8,128)(2,1)}) %all-gather.9.cloned.1.call-update) | async-done | bytes 3604496 | tf_op jit(solution)/shard_map/all_gather | solution.py:292
  109.5 1.9 maximum_select_fusion.3
  112.2 20.5 %collective-permute-done.4 = bf16[1,2,2,1,192,640]{5,4,3,2,1,0:T(8,128)(2,1)} collective-permute-done((bf16[1,2,2,1,192,640]{5,4,3,2,1,0:T(8,128)(2,1)}, bf16[1,2,2,1,192,640]{5,4,3,2,1,0:T(8,128)(2,1)}, u32[]{:S(2)}, u32[]{:S(2)}) %collective-permute-start.4) | collective-permute-done | bytes 983072 | tf_op jit(solution)/shard_map/ppermute | solution.py:222
  132.8 3.2 maximum_select_fusion.2
  139.8 34.7 %collective-permute-done.9 = bf16[1,2,2,2,192,640]{5,4,1,2,3,0:T(8,128)(2,1)} collective-permute-done((bf16[1,2,2,2,192,640]{5,4,1,2,3,0:T(8,128)(2,1)S(1)}, bf16[1,2,2,2,192,640]{5,4,1,2,3,0:T(8,128)(2,1)}, u32[]{:S(2)}, u32[]{:S(2)}) %collective-permute-start.9) | collective-permute-done | bytes 1966112 | tf_op jit(solution)/shard_map/ppermute | solution.py:222
  174.5 2.9 maximum_select_fusion.1
  177.4 2.2 copy.136
  180.4 5.8 maximum_select_fusion
  187.5 3.8 broadcast_select_fusion.6
  197.6 5.3 broadcast_select_fusion.4
  202.9 8.8 %broadcast_select_fusion = (bf16[16,256,640]{2,1,0:T(8,128)(2,1)}, bf16[16,256,640]{2,1,0:T(8,128)(2,1)}) fusion(pred[]{:T(512)S(6)} %not.2, bf16[16,192,640]{2,1,0:T(8,128)(2,1)} %bitcast.54, bf16[16,192,640]{2,1,0:T(8,128)(2,1)} %bitcast.44, bf16[16,192,640]{2,1,0:T(8,128)(2,1)} %collective-permute-done.11, ...), kind=kLoop, calls=%fused_computation.6 | loop fusion | flops 26214400 | bytes 26214402 | tf_op jit(solution)/shard_map/jit(_where)/select_n | solution.py:307
  213.7 3.0 broadcast_select_fusion.10
  216.7 24.9 %all-gather.5.cloned.1.call-done = bf16[16,3,64,512]{3,2,1,0:T(8,128)(2,1)} async-done(((bf16[1,3,64,512]{3,2,1,0:T(8,128)(2,1)}), bf16[16,3,64,512]{3,2,1,0:T(8,128)(2,1)}) %all-gather.5.cloned.1.call-update) | async-done | bytes 3145744 | tf_op jit(solution)/shard_map/all_gather | solution.py:99
  241.6 3.9 copy.124
  245.6 6.0 fusion.183
  251.5 4.0 fusion.184
  257.2 1.9 fusion.159
  269.2 42.1 %all-gather.7.cloned.1.call-done = bf16[16,3,64,512]{3,2,1,0:T(8,128)(2,1)} async-done(((bf16[1,3,64,512]{3,2,1,0:T(8,128)(2,1)}), bf16[16,3,64,512]{3,2,1,0:T(8,128)(2,1)}) %all-gather.7.cloned.1.call-update) | async-done | bytes 3145744 | tf_op jit(solution)/shard_map/all_gather | solution.py:99
  311.4 3.9 copy.139
  315.3 6.4 fusion.185
  321.7 3.1 fusion.186
  326.2 1.9 fusion.160
  331.7 2.5 fusion.63
  334.3 2.1 multiply_reduce_fusion.13
  336.3 1.9 convolution_convert_fusion.1
  340.8 2.4 broadcast_select_fusion.3
  348.7 1.8 copy.167
  351.9 2.6 fusion.49
  356.5 3.4 select_add_fusion.1
  363.9 25.0 %collective-permute-done.13 = bf16[2,2,2,1,96,640]{5,4,3,2,1,0:T(8,128)(2,1)S(1)} collective-permute-done((bf16[2,2,2,1,96,640]{5,4,3,2,1,0:T(8,128)(2,1)S(1)}, bf16[2,2,2,1,96,640]{5,4,3,2,1,0:T(8,128)(2,1)S(1)}, u32[]{:S(2)}, u32[]{:S(2)}) %collective-permute-start.13) | collective-permute-done | bytes 983072 | tf_op jit(solution)/shard_map/ppermute | solution.py:225
  393.2 1.7 convolution_convert_fusion.9
  394.9 25.1 %reduce-scatter.3.cloned.1.call-done = bf16[192,512]{1,0:T(8,128)(2,1)} async-done(((bf16[3072,512]{1,0:T(8,128)(2,1)}), bf16[192,512]{1,0:T(8,128)(2,1)}) %reduce-scatter.3.cloned.1.call-update) | async-done | bytes 196624 | tf_op jit(solution)/shard_map/reduce_scatter | solution.py:108
  428.3 3.5 fusion.62
  431.9 2.6 convolution_convert_fusion.4
  439.5 1.9 broadcast_select_fusion.9
  441.7 1.9 convolution_convert_fusion
  443.7 2.4 broadcast_select_fusion.2
  447.4 2.0 multiply_reduce_fusion.8
  460.7 6.8 %collective-permute-done.24 = bf16[1,2,2,2,40,640]{5,4,3,2,1,0:T(8,128)(2,1)S(1)} collective-permute-done((bf16[1,2,2,2,40,640]{5,4,3,2,1,0:T(8,128)(2,1)S(1)}, bf16[1,2,2,2,40,640]{5,4,3,2,1,0:T(8,128)(2,1)S(1)}, u32[]{:S(2)}, u32[]{:S(2)}) %collective-permute-start.24) | collective-permute-done | bytes 409632 | tf_op jit(solution)/shard_map/ppermute | solution.py:222
  470.6 2.9 collective-permute-done.25
  481.3 1.9 copy.168
  484.9 2.4 fusion.46
  490.5 1.7 convolution_convert_fusion.8
  494.4 3.5 select_add_fusion
  498.9 2.2 collective-permute-start.34
  503.8 25.9 %collective-permute-done.27 = bf16[2,2,2,1,96,640]{5,4,3,2,1,0:T(8,128)(2,1)S(1)} collective-permute-done((bf16[2,2,2,1,96,640]{5,4,3,2,1,0:T(8,128)(2,1)S(1)}, bf16[2,2,2,1,96,640]{5,4,3,2,1,0:T(8,128)(2,1)S(1)}, u32[]{:S(2)}, u32[]{:S(2)}) %collective-permute-start.27) | collective-permute-done | bytes 983072 | tf_op jit(solution)/shard_map/ppermute | solution.py:225
  529.9 1.7 collective-permute-start.28
  534.1 4.7 collective-permute-done.28
  541.7 14.7 %reduce-scatter.5.cloned.1.call-done = bf16[192,512]{1,0:T(8,128)(2,1)} async-done(((bf16[3072,512]{1,0:T(8,128)(2,1)}), bf16[192,512]{1,0:T(8,128)(2,1)}) %reduce-scatter.5.cloned.1.call-update) | async-done | bytes 196624 | tf_op jit(solution)/shard_map/reduce_scatter | solution.py:108
  558.2 1.8 fusion.162
  568.8 5.6 collective-permute-done.48
  575.8 5.8 collective-permute-done.46
  583.8 5.9 collective-permute-done.47
  593.6 9.1 %collective-permute-done.41 = bf16[1,2,2,2,40,640]{5,4,3,2,1,0:T(8,128)(2,1)S(1)} collective-permute-done((bf16[1,2,2,2,40,640]{5,4,3,2,1,0:T(8,128)(2,1)S(1)}, bf16[1,2,2,2,40,640]{5,4,3,2,1,0:T(8,128)(2,1)S(1)}, u32[]{:S(2)}, u32[]{:S(2)}) %collective-permute-start.41) | collective-permute-done | bytes 409632 | tf_op jit(solution)/shard_map/ppermute | solution.py:222
  603.9 2.3 collective-permute-done.37
  606.5 3.6 collective-permute-done.42
  611.5 3.5 collective-permute-done.43
  615.2 2.3 collective-permute-start.44
  617.5 3.1 collective-permute-done.39
  620.8 5.0 collective-permute-done.40
  (708 shorter events, 138.6 us)
Async XLA Ops:
  7.2 130.4 %copy-start = (s32[3,1,128]{2,1,0:T(1,128)S(1)}, s32[3,1,128]{2,1,0:T(1,128)}, u32[]{:S(2)}) copy-start(s32[3,1,128]{2,1,0:T(1,128)} %param.8) | copy-start | bytes 4612
  7.2 99.5 %all-gather.9.cloned.1.call-start = ((), (), s32[]{:S(2)}) async-start(), calls=%async_computation.6 | async-start | bytes 3829760 | tf_op jit(solution)/shard_map/all_gather | solution.py:292
  8.9 232.7 %all-gather.5.cloned.1.call-start = ((), (), s32[]{:S(2)}) async-start(), calls=%async_computation.2 | async-start | bytes 3342336 | tf_op jit(solution)/shard_map/all_gather | solution.py:99
  11.2 25.9 %collective-permute-start.6 = (bf16[1,1,1,1,192,640]{5,4,1,2,3,0:T(8,128)(2,1)S(1)}, bf16[1,1,1,1,192,640]{5,4,1,2,3,0:T(8,128)(2,1)S(1)}, u32[]{:S(2)}, u32[]{:S(2)}) collective-permute-start(bf16[1,1,1,1,192,640]{5,4,1,2,3,0:T(8,128)(2,1)S(1)} %get-tuple-element.184), channel_id=1, source_target_pairs={{0,4},{1,5},{2,6},{3,7},{4,0},{5,1},{6,2},{7,3},{8,12},{9,13},{10,... | collective-permute-start | bytes 737288 | tf_op jit(solution)/shard_map/ppermute | solution.py:225
  15.3 26.6 %collective-permute-start.2 = (bf16[1,1,1,1,192,640]{5,4,1,3,2,0:T(8,128)(2,1)S(1)}, bf16[1,1,1,1,192,640]{5,4,1,3,2,0:T(8,128)(2,1)S(1)}, u32[]{:S(2)}, u32[]{:S(2)}) collective-permute-start(bf16[1,1,1,1,192,640]{5,4,1,3,2,0:T(8,128)(2,1)S(1)} %get-tuple-element.183), channel_id=1, source_target_pairs={{0,4},{1,5},{2,6},{3,7},{4,0},{5,1},{6,2},{7,3},{8,12},{9,13},{10,... | collective-permute-start | bytes 737288 | tf_op jit(solution)/shard_map/ppermute | solution.py:225
  37.1 21.1 %collective-permute-start.7 = (bf16[1,2,1,1,192,640]{5,4,1,2,3,0:T(8,128)(2,1)S(1)}, bf16[1,2,1,1,192,640]{5,4,1,2,3,0:T(8,128)(2,1)S(1)}, u32[]{:S(2)}, u32[]{:S(2)}) collective-permute-start(bf16[1,2,1,1,192,640]{5,4,1,2,3,0:T(8,128)(2,1)S(1)} %maximum_select_fusion.7), channel_id=1, source_target_pairs={{0,2},{1,3},{2,0},{3,1},{4,6},{5,7},{6,4},{7,5},{8,10},{9,11},{10,... | collective-permute-start | bytes 1474568 | tf_op jit(solution)/shard_map/ppermute | solution.py:225
  42.8 63.9 %collective-permute-start.3 = (bf16[1,2,1,1,192,640]{5,4,1,3,2,0:T(8,128)(2,1)}, bf16[1,2,1,1,192,640]{5,4,1,3,2,0:T(8,128)(2,1)S(1)}, u32[]{:S(2)}, u32[]{:S(2)}) collective-permute-start(bf16[1,2,1,1,192,640]{5,4,1,3,2,0:T(8,128)(2,1)} %fusion.80), channel_id=1, source_target_pairs={{0,2},{1,3},{2,0},{3,1},{4,6},{5,7},{6,4},{7,5},{8,10},{9,11},{10,... | collective-permute-start | bytes 1474568 | tf_op jit(solution)/shard_map/ppermute | solution.py:225
  59.3 50.1 %collective-permute-start.8 = (bf16[1,2,2,1,192,640]{5,4,1,2,3,0:T(8,128)(2,1)}, bf16[1,2,2,1,192,640]{5,4,1,2,3,0:T(8,128)(2,1)}, u32[]{:S(2)}, u32[]{:S(2)}) collective-permute-start(bf16[1,2,2,1,192,640]{5,4,1,2,3,0:T(8,128)(2,1)} %maximum_select_fusion.5), channel_id=1, source_target_pairs={{0,1},{1,0},{2,3},{3,2},{4,5},{5,4},{6,7},{7,6},{8,9},{9,8},{10,11... | collective-permute-start | bytes 2949128 | tf_op jit(solution)/shard_map/ppermute | solution.py:225
  106.7 79.5 %collective-permute-start.1 = (bf16[16,176,640]{2,1,0:T(8,128)(2,1)}, bf16[16,176,640]{2,1,0:T(8,128)(2,1)}, u32[]{:S(2)}, u32[]{:S(2)}) collective-permute-start(bf16[16,176,640]{2,1,0:T(8,128)(2,1)} %bitcast.377), channel_id=1, source_target_pairs={{0,16},{16,0},{1,17},{17,1},{2,18},{18,2},{3,19},{19,3},{4,20},{20... | collective-permute-start | bytes 10813448 | tf_op jit(solution)/shard_map/ppermute | solution.py:40
  107.9 24.9 %collective-permute-start.4 = (bf16[1,2,2,1,192,640]{5,4,3,2,1,0:T(8,128)(2,1)}, bf16[1,2,2,1,192,640]{5,4,3,2,1,0:T(8,128)(2,1)}, u32[]{:S(2)}, u32[]{:S(2)}) collective-permute-start(bf16[1,2,2,1,192,640]{5,4,3,2,1,0:T(8,128)(2,1)} %copy.135), channel_id=1, source_target_pairs={{0,8},{8,0},{1,9},{9,1},{2,10},{10,2},{3,11},{11,3},{4,12},{12,4},... | collective-permute-start | bytes 2949128 | tf_op jit(solution)/shard_map/ppermute | solution.py:222
  111.4 63.1 %collective-permute-start.9 = (bf16[1,2,2,2,192,640]{5,4,1,2,3,0:T(8,128)(2,1)S(1)}, bf16[1,2,2,2,192,640]{5,4,1,2,3,0:T(8,128)(2,1)}, u32[]{:S(2)}, u32[]{:S(2)}) collective-permute-start(bf16[1,2,2,2,192,640]{5,4,1,2,3,0:T(8,128)(2,1)S(1)} %maximum_select_fusion.3), channel_id=1, source_target_pairs={{0,8},{8,0},{1,9},{9,1},{2,10},{10,2},{3,11},{11,3},{4,12},{12,4},... | collective-permute-start | bytes 5898248 | tf_op jit(solution)/shard_map/ppermute | solution.py:222
  136.0 44.4 %collective-permute-start.5 = (bf16[2,2,2,1,192,640]{5,4,3,2,1,0:T(8,128)(2,1)}, bf16[2,2,2,1,192,640]{5,4,3,2,1,0:T(8,128)(2,1)}, u32[]{:S(2)}, u32[]{:S(2)}) collective-permute-start(bf16[2,2,2,1,192,640]{5,4,3,2,1,0:T(8,128)(2,1)} %maximum_select_fusion.2), channel_id=1, source_target_pairs={{0,1},{1,0},{2,3},{3,2},{4,5},{5,4},{6,7},{7,6},{8,9},{9,8},{10,11... | collective-permute-start | bytes 5898248 | tf_op jit(solution)/shard_map/ppermute | solution.py:225
  137.5 1.6 collective-permute-start
  137.6 55.2 %copy-start.152 = (f32[128]{0:T(128)}, f32[128]{0:T(128)S(1)}, u32[]{:S(2)}) copy-start(f32[128]{0:T(128)S(1)} %fusion.140) | copy-start | bytes 1540
  139.0 38.4 %copy-start.67 = (bf16[3,64,640]{2,1,0:T(8,128)(2,1)}, bf16[3,64,640]{2,1,0:T(8,128)(2,1)S(1)}, u32[]{:S(2)}) copy-start(bf16[3,64,640]{2,1,0:T(8,128)(2,1)S(1)} %collective-permute-done) | copy-start | bytes 737284
  179.6 17.9 %collective-permute-start.11 = (bf16[16,192,640]{2,1,0:T(8,128)(2,1)}, bf16[16,192,640]{2,1,0:T(8,128)(2,1)}, u32[]{:S(2)}, u32[]{:S(2)}) collective-permute-start(bf16[16,192,640]{2,1,0:T(8,128)(2,1)} %bitcast.54), channel_id=1, source_target_pairs={{0,16},{16,0},{1,17},{17,1},{2,18},{18,2},{3,19},{19,3},{4,20},{20... | collective-permute-start | bytes 11796488 | tf_op jit(solution)/shard_map/ppermute | solution.py:40
  186.1 16.7 %collective-permute-start.10 = (bf16[16,192,640]{2,1,0:T(8,128)(2,1)}, bf16[16,192,640]{2,1,0:T(8,128)(2,1)}, u32[]{:S(2)}, u32[]{:S(2)}) collective-permute-start(bf16[16,192,640]{2,1,0:T(8,128)(2,1)} %bitcast.44), channel_id=1, source_target_pairs={{0,16},{16,0},{1,17},{17,1},{2,18},{18,2},{3,19},{19,3},{4,20},{20... | collective-permute-start | bytes 11796488 | tf_op jit(solution)/shard_map/ppermute | solution.py:40
  194.1 117.3 %all-gather.7.cloned.1.call-start = ((), (), s32[]{:S(2)}) async-start(), calls=%async_computation.3 | async-start | bytes 3342336 | tf_op jit(solution)/shard_map/all_gather | solution.py:99
  194.5 51.1 %copy-start.148 = (s32[3,256]{1,0:T(4,128)}, s32[3,256]{1,0:T(4,128)S(1)}, u32[]{:S(2)}) copy-start(s32[3,256]{1,0:T(4,128)S(1)} %tile.19) | copy-start | bytes 9220
  196.4 49.1 %copy-start.81 = (pred[256,1024]{1,0:T(8,128)(4,1)}, pred[256,1024]{1,0:T(8,128)(4,1)S(1)}, u32[]{:S(2)}) copy-start(pred[256,1024]{1,0:T(8,128)(4,1)S(1)} %get-tuple-element.203) | copy-start | bytes 786436
  212.3 33.3 %copy-start.82 = (bf16[3,4,64,128]{3,2,1,0:T(8,128)(2,1)}, bf16[3,4,64,128]{3,2,1,0:T(8,128)(2,1)S(1)}, u32[]{:S(2)}) copy-start(bf16[3,4,64,128]{3,2,1,0:T(8,128)(2,1)S(1)} %copy.123) | copy-start | bytes 589828
  213.7 51.4 %copy-start.118 = (f32[256]{0:T(256)}, f32[256]{0:T(256)S(1)}, u32[]{:S(2)}) copy-start(f32[256]{0:T(256)S(1)} %get-tuple-element.195) | copy-start | bytes 3076
  216.7 38.9 %copy-start.20 = (bf16[16,64,640]{2,1,0:T(8,128)(2,1)}, bf16[16,64,640]{2,1,0:T(8,128)(2,1)S(1)}, u32[]{:S(2)}) copy-start(bf16[16,64,640]{2,1,0:T(8,128)(2,1)S(1)} %get-tuple-element.102) | copy-start | bytes 3932164
  267.0 153.0 %reduce-scatter.3.cloned.1.call-start = ((), (), s32[]{:S(2)}) async-start(), calls=%async_computation.4 | async-start | bytes 3342336 | tf_op jit(solution)/shard_map/reduce_scatter | solution.py:108
  343.2 13.0 %collective-permute-start.12 = (bf16[16,192,640]{2,1,0:T(8,128)(2,1)}, bf16[16,192,640]{2,1,0:T(8,128)(2,1)}, u32[]{:S(2)}, u32[]{:S(2)}) collective-permute-start(bf16[16,192,640]{2,1,0:T(8,128)(2,1)} %broadcast_select_fusion.3), channel_id=1, source_target_pairs={{0,16},{16,0},{1,17},{17,1},{2,18},{18,2},{3,19},{19,3},{4,20},{20... | collective-permute-start | bytes 11796488 | tf_op jit(solution)/shard_map/ppermute | solution.py:40
  350.5 205.9 %reduce-scatter.5.cloned.1.call-start = ((), (), s32[]{:S(2)}) async-start(), calls=%async_computation.5 | async-start | bytes 3342336 | tf_op jit(solution)/shard_map/reduce_scatter | solution.py:108
  360.1 28.8 %collective-permute-start.13 = (bf16[2,2,2,1,96,640]{5,4,3,2,1,0:T(8,128)(2,1)S(1)}, bf16[2,2,2,1,96,640]{5,4,3,2,1,0:T(8,128)(2,1)S(1)}, u32[]{:S(2)}, u32[]{:S(2)}) collective-permute-start(bf16[2,2,2,1,96,640]{5,4,3,2,1,0:T(8,128)(2,1)S(1)} %broadcast_select_fusion.17), channel_id=1, source_target_pairs={{0,1},{1,0},{2,3},{3,2},{4,5},{5,4},{6,7},{7,6},{8,9},{9,8},{10,11... | collective-permute-start | bytes 2949128 | tf_op jit(solution)/shard_map/ppermute | solution.py:225
  361.0 30.5 %collective-permute-start.15 = (bf16[1,2,2,2,96,640]{5,4,3,2,1,0:T(8,128)(2,1)S(1)}, bf16[1,2,2,2,96,640]{5,4,3,2,1,0:T(8,128)(2,1)S(1)}, u32[]{:S(2)}, u32[]{:S(2)}) collective-permute-start(bf16[1,2,2,2,96,640]{5,4,3,2,1,0:T(8,128)(2,1)S(1)} %bitcast.409), channel_id=1, source_target_pairs={{0,8},{8,0},{1,9},{9,1},{2,10},{10,2},{3,11},{11,3},{4,12},{12,4},... | collective-permute-start | bytes 2949128 | tf_op jit(solution)/shard_map/ppermute | solution.py:222
  389.9 31.1 %collective-permute-start.14 = (bf16[1,2,2,1,96,640]{5,4,3,2,1,0:T(8,128)(2,1)}, bf16[1,2,2,1,96,640]{5,4,3,2,1,0:T(8,128)(2,1)}, u32[]{:S(2)}, u32[]{:S(2)}) collective-permute-start(bf16[1,2,2,1,96,640]{5,4,3,2,1,0:T(8,128)(2,1)} %broadcast_select_fusion.23), channel_id=1, source_target_pairs={{0,8},{8,0},{1,9},{9,1},{2,10},{10,2},{3,11},{11,3},{4,12},{12,4},... | collective-permute-start | bytes 1474568 | tf_op jit(solution)/shard_map/ppermute | solution.py:222
  392.6 29.6 %collective-permute-start.16 = (bf16[1,2,2,1,96,640]{5,4,3,2,1,0:T(8,128)(2,1)}, bf16[1,2,2,1,96,640]{5,4,3,2,1,0:T(8,128)(2,1)}, u32[]{:S(2)}, u32[]{:S(2)}) collective-permute-start(bf16[1,2,2,1,96,640]{5,4,3,2,1,0:T(8,128)(2,1)} %broadcast_select_fusion.21), channel_id=1, source_target_pairs={{0,1},{1,0},{2,3},{3,2},{4,5},{5,4},{6,7},{7,6},{8,9},{9,8},{10,11... | collective-permute-start | bytes 1474568 | tf_op jit(solution)/shard_map/ppermute | solution.py:225
  435.2 14.5 %collective-permute-start.17 = (bf16[1,2,1,1,96,640]{5,4,3,2,1,0:T(8,128)(2,1)}, bf16[1,2,1,1,96,640]{5,4,3,2,1,0:T(8,128)(2,1)}, u32[]{:S(2)}, u32[]{:S(2)}) collective-permute-start(bf16[1,2,1,1,96,640]{5,4,3,2,1,0:T(8,128)(2,1)} %broadcast_select_fusion.33), channel_id=1, source_target_pairs={{0,2},{1,3},{2,0},{3,1},{4,6},{5,7},{6,4},{7,5},{8,10},{9,11},{10,... | collective-permute-start | bytes 737288 | tf_op jit(solution)/shard_map/ppermute | solution.py:225
  437.0 15.8 %collective-permute-start.19 = (bf16[1,2,1,1,96,640]{5,4,3,2,1,0:T(8,128)(2,1)}, bf16[1,2,1,1,96,640]{5,4,3,2,1,0:T(8,128)(2,1)}, u32[]{:S(2)}, u32[]{:S(2)}) collective-permute-start(bf16[1,2,1,1,96,640]{5,4,3,2,1,0:T(8,128)(2,1)} %broadcast_select_fusion.32), channel_id=1, source_target_pairs={{0,2},{1,3},{2,0},{3,1},{4,6},{5,7},{6,4},{7,5},{8,10},{9,11},{10,... | collective-permute-start | bytes 737288 | tf_op jit(solution)/shard_map/ppermute | solution.py:225
  441.4 12.4 %collective-permute-start.21 = (bf16[16,88,640]{2,1,0:T(8,128)(2,1)S(1)}, bf16[16,88,640]{2,1,0:T(8,128)(2,1)S(1)}, u32[]{:S(2)}, u32[]{:S(2)}) collective-permute-start(bf16[16,88,640]{2,1,0:T(8,128)(2,1)S(1)} %broadcast_select_fusion.9), channel_id=1, source_target_pairs={{0,16},{16,0},{1,17},{17,1},{2,18},{18,2},{3,19},{19,3},{4,20},{20... | collective-permute-start | bytes 5406728 | tf_op jit(solution)/shard_map/ppermute | solution.py:40
  447.2 47.2 %collective-permute-start.26 = (bf16[16,192,640]{2,1,0:T(8,128)(2,1)}, bf16[16,192,640]{2,1,0:T(8,128)(2,1)}, u32[]{:S(2)}, u32[]{:S(2)}) collective-permute-start(bf16[16,192,640]{2,1,0:T(8,128)(2,1)} %broadcast_select_fusion.2), channel_id=1, source_target_pairs={{0,16},{16,0},{1,17},{17,1},{2,18},{18,2},{3,19},{19,3},{4,20},{20... | collective-permute-start | bytes 11796488 | tf_op jit(solution)/shard_map/ppermute | solution.py:40
  451.5 9.1 %collective-permute-start.18 = (bf16[1,1,1,1,96,640]{5,4,3,2,1,0:T(8,128)(2,1)S(1)}, bf16[1,1,1,1,96,640]{5,4,3,2,1,0:T(8,128)(2,1)S(1)}, u32[]{:S(2)}, u32[]{:S(2)}) collective-permute-start(bf16[1,1,1,1,96,640]{5,4,3,2,1,0:T(8,128)(2,1)S(1)} %broadcast_select_fusion.52), channel_id=1, source_target_pairs={{0,4},{1,5},{2,6},{3,7},{4,0},{5,1},{6,2},{7,3},{8,12},{9,13},{10,... | collective-permute-start | bytes 368648 | tf_op jit(solution)/shard_map/ppermute | solution.py:225
  454.8 13.4 %collective-permute-start.22 = (bf16[2,2,2,1,48,640]{5,4,3,2,1,0:T(8,128)(2,1)S(1)}, bf16[2,2,2,1,48,640]{5,4,3,2,1,0:T(8,128)(2,1)S(1)}, u32[]{:S(2)}, u32[]{:S(2)}) collective-permute-start(bf16[2,2,2,1,48,640]{5,4,3,2,1,0:T(8,128)(2,1)S(1)} %broadcast_select_fusion.19), channel_id=1, source_target_pairs={{0,1},{1,0},{2,3},{3,2},{4,5},{5,4},{6,7},{7,6},{8,9},{9,8},{10,11... | collective-permute-start | bytes 1474568 | tf_op jit(solution)/shard_map/ppermute | solution.py:225
  456.4 11.1 %collective-permute-start.24 = (bf16[1,2,2,2,40,640]{5,4,3,2,1,0:T(8,128)(2,1)S(1)}, bf16[1,2,2,2,40,640]{5,4,3,2,1,0:T(8,128)(2,1)S(1)}, u32[]{:S(2)}, u32[]{:S(2)}) collective-permute-start(bf16[1,2,2,2,40,640]{5,4,3,2,1,0:T(8,128)(2,1)S(1)} %bitcast.431), channel_id=1, source_target_pairs={{0,8},{8,0},{1,9},{9,1},{2,10},{10,2},{3,11},{11,3},{4,12},{12,4},... | collective-permute-start | bytes 1228808 | tf_op jit(solution)/shard_map/ppermute | solution.py:222
  457.9 12.1 %collective-permute-start.20 = (bf16[1,1,1,1,96,640]{5,4,3,2,1,0:T(8,128)(2,1)S(1)}, bf16[1,1,1,1,96,640]{5,4,3,2,1,0:T(8,128)(2,1)S(1)}, u32[]{:S(2)}, u32[]{:S(2)}) collective-permute-start(bf16[1,1,1,1,96,640]{5,4,3,2,1,0:T(8,128)(2,1)S(1)} %broadcast_select_fusion.51), channel_id=1, source_target_pairs={{0,4},{1,5},{2,6},{3,7},{4,0},{5,1},{6,2},{7,3},{8,12},{9,13},{10,... | collective-permute-start | bytes 368648 | tf_op jit(solution)/shard_map/ppermute | solution.py:225
  467.6 5.9 collective-permute-start.25
  468.3 6.9 %collective-permute-start.23 = (bf16[1,2,2,1,48,640]{5,4,3,2,1,0:T(8,128)(2,1)S(1)}, bf16[1,2,2,1,48,640]{5,4,3,2,1,0:T(8,128)(2,1)S(1)}, u32[]{:S(2)}, u32[]{:S(2)}) collective-permute-start(bf16[1,2,2,1,48,640]{5,4,3,2,1,0:T(8,128)(2,1)S(1)} %broadcast_select_fusion.29), channel_id=1, source_target_pairs={{0,8},{8,0},{1,9},{9,1},{2,10},{10,2},{3,11},{11,3},{4,12},{12,4},... | collective-permute-start | bytes 737288 | tf_op jit(solution)/shard_map/ppermute | solution.py:222
  483.3 19.5 %collective-permute-start.31 = (bf16[1,2,1,1,48,640]{5,4,3,2,1,0:T(8,128)(2,1)S(1)}, bf16[1,2,1,1,48,640]{5,4,3,2,1,0:T(8,128)(2,1)S(1)}, u32[]{:S(2)}, u32[]{:S(2)}) collective-permute-start(bf16[1,2,1,1,48,640]{5,4,3,2,1,0:T(8,128)(2,1)S(1)} %broadcast_select_fusion.48), channel_id=1, source_target_pairs={{0,2},{1,3},{2,0},{3,1},{4,6},{5,7},{6,4},{7,5},{8,10},{9,11},{10,... | collective-permute-start | bytes 368648 | tf_op jit(solution)/shard_map/ppermute | solution.py:225
  489.6 4.7 collective-permute-start.33
  498.2 31.5 %collective-permute-start.27 = (bf16[2,2,2,1,96,640]{5,4,3,2,1,0:T(8,128)(2,1)S(1)}, bf16[2,2,2,1,96,640]{5,4,3,2,1,0:T(8,128)(2,1)S(1)}, u32[]{:S(2)}, u32[]{:S(2)}) collective-permute-start(bf16[2,2,2,1,96,640]{5,4,3,2,1,0:T(8,128)(2,1)S(1)} %broadcast_select_fusion.16), channel_id=1, source_target_pairs={{0,1},{1,0},{2,3},{3,2},{4,5},{5,4},{6,7},{7,6},{8,9},{9,8},{10,11... | collective-permute-start | bytes 2949128 | tf_op jit(solution)/shard_map/ppermute | solution.py:225
  498.9 33.9 %collective-permute-start.34 = (bf16[1,1,1,1,40,640]{5,4,3,2,1,0:T(8,128)(2,1)S(1)}, bf16[1,1,1,1,40,640]{5,4,3,2,1,0:T(8,128)(2,1)S(1)}, u32[]{:S(2)}, u32[]{:S(2)}) collective-permute-start(bf16[1,1,1,1,40,640]{5,4,3,2,1,0:T(8,128)(2,1)S(1)} %broadcast_select_fusion.64), channel_id=1, source_target_pairs={{0,4},{1,5},{2,6},{3,7},{4,0},{5,1},{6,2},{7,3},{8,12},{9,13},{10,... | collective-permute-start | bytes 153608 | tf_op jit(solution)/shard_map/ppermute | solution.py:225
  501.3 30.4 %collective-permute-start.29 = (bf16[1,2,2,2,96,640]{5,4,3,2,1,0:T(8,128)(2,1)S(1)}, bf16[1,2,2,2,96,640]{5,4,3,2,1,0:T(8,128)(2,1)S(1)}, u32[]{:S(2)}, u32[]{:S(2)}) collective-permute-start(bf16[1,2,2,2,96,640]{5,4,3,2,1,0:T(8,128)(2,1)S(1)} %bitcast.410), channel_id=1, source_target_pairs={{0,8},{8,0},{1,9},{9,1},{2,10},{10,2},{3,11},{11,3},{4,12},{12,4},... | collective-permute-start | bytes 2949128 | tf_op jit(solution)/shard_map/ppermute | solution.py:222
  502.9 30.6 %collective-permute-start.32 = (bf16[1,1,1,1,48,640]{5,4,3,2,1,0:T(8,128)(2,1)S(1)}, bf16[1,1,1,1,48,640]{5,4,3,2,1,0:T(8,128)(2,1)S(1)}, u32[]{:S(2)}, u32[]{:S(2)}) collective-permute-start(bf16[1,1,1,1,48,640]{5,4,3,2,1,0:T(8,128)(2,1)S(1)} %broadcast_select_fusion.62), channel_id=1, source_target_pairs={{0,4},{1,5},{2,6},{3,7},{4,0},{5,1},{6,2},{7,3},{8,12},{9,13},{10,... | collective-permute-start | bytes 184328 | tf_op jit(solution)/shard_map/ppermute | solution.py:225
  529.9 8.9 %collective-permute-start.28 = (bf16[1,2,2,1,96,640]{5,4,3,2,1,0:T(8,128)(2,1)S(1)}, bf16[1,2,2,1,96,640]{5,4,3,2,1,0:T(8,128)(2,1)S(1)}, u32[]{:S(2)}, u32[]{:S(2)}) collective-permute-start(bf16[1,2,2,1,96,640]{5,4,3,2,1,0:T(8,128)(2,1)S(1)} %broadcast_select_fusion.22), channel_id=1, source_target_pairs={{0,8},{8,0},{1,9},{9,1},{2,10},{10,2},{3,11},{11,3},{4,12},{12,4},... | collective-permute-start | bytes 1474568 | tf_op jit(solution)/shard_map/ppermute | solution.py:222
  531.9 8.9 %collective-permute-start.30 = (bf16[1,2,2,1,96,640]{5,4,3,2,1,0:T(8,128)(2,1)S(1)}, bf16[1,2,2,1,96,640]{5,4,3,2,1,0:T(8,128)(2,1)S(1)}, u32[]{:S(2)}, u32[]{:S(2)}) collective-permute-start(bf16[1,2,2,1,96,640]{5,4,3,2,1,0:T(8,128)(2,1)S(1)} %broadcast_select_fusion.20), channel_id=1, source_target_pairs={{0,1},{1,0},{2,3},{3,2},{4,5},{5,4},{6,7},{7,6},{8,9},{9,8},{10,11... | collective-permute-start | bytes 1474568 | tf_op jit(solution)/shard_map/ppermute | solution.py:225
  562.1 19.9 %collective-permute-start.35 = (bf16[3,64,640]{2,1,0:T(8,128)(2,1)}, bf16[3,64,640]{2,1,0:T(8,128)(2,1)}, u32[]{:S(2)}, u32[]{:S(2)}) collective-permute-start(bf16[3,64,640]{2,1,0:T(8,128)(2,1)} %bitcast.138), channel_id=1, source_target_pairs={{0,16},{16,0},{1,17},{17,1},{2,18},{18,2},{3,19},{19,3},{4,20},{20... | collective-permute-start | bytes 737288 | tf_op jit(solution)/shard_map/ppermute | solution.py:40
  565.5 8.8 %collective-permute-start.48 = (bf16[1,2,1,1,96,640]{5,4,3,2,1,0:T(8,128)(2,1)S(1)}, bf16[1,2,1,1,96,640]{5,4,3,2,1,0:T(8,128)(2,1)S(1)}, u32[]{:S(2)}, u32[]{:S(2)}) collective-permute-start(bf16[1,2,1,1,96,640]{5,4,3,2,1,0:T(8,128)(2,1)S(1)} %broadcast_select_fusion.30), channel_id=1, source_target_pairs={{0,2},{1,3},{2,0},{3,1},{4,6},{5,7},{6,4},{7,5},{8,10},{9,11},{10,... | collective-permute-start | bytes 737288 | tf_op jit(solution)/shard_map/ppermute | solution.py:225
  567.1 22.7 %collective-permute-start.36 = (bf16[16,88,640]{2,1,0:T(8,128)(2,1)S(1)}, bf16[16,88,640]{2,1,0:T(8,128)(2,1)S(1)}, u32[]{:S(2)}, u32[]{:S(2)}) collective-permute-start(bf16[16,88,640]{2,1,0:T(8,128)(2,1)S(1)} %broadcast_select_fusion.8), channel_id=1, source_target_pairs={{0,16},{16,0},{1,17},{17,1},{2,18},{18,2},{3,19},{19,3},{4,20},{20... | collective-permute-start | bytes 5406728 | tf_op jit(solution)/shard_map/ppermute | solution.py:40
  567.7 13.8 %collective-permute-start.46 = (bf16[1,2,1,1,96,640]{5,4,3,2,1,0:T(8,128)(2,1)S(1)}, bf16[1,2,1,1,96,640]{5,4,3,2,1,0:T(8,128)(2,1)S(1)}, u32[]{:S(2)}, u32[]{:S(2)}) collective-permute-start(bf16[1,2,1,1,96,640]{5,4,3,2,1,0:T(8,128)(2,1)S(1)} %broadcast_select_fusion.31), channel_id=1, source_target_pairs={{0,2},{1,3},{2,0},{3,1},{4,6},{5,7},{6,4},{7,5},{8,10},{9,11},{10,... | collective-permute-start | bytes 737288 | tf_op jit(solution)/shard_map/ppermute | solution.py:225
  574.4 9.3 %collective-permute-start.49 = (bf16[1,1,1,1,96,640]{5,4,3,2,1,0:T(8,128)(2,1)S(1)}, bf16[1,1,1,1,96,640]{5,4,3,2,1,0:T(8,128)(2,1)S(1)}, u32[]{:S(2)}, u32[]{:S(2)}) collective-permute-start(bf16[1,1,1,1,96,640]{5,4,3,2,1,0:T(8,128)(2,1)S(1)} %broadcast_select_fusion.49), channel_id=1, source_target_pairs={{0,4},{1,5},{2,6},{3,7},{4,0},{5,1},{6,2},{7,3},{8,12},{9,13},{10,... | collective-permute-start | bytes 368648 | tf_op jit(solution)/shard_map/ppermute | solution.py:225
  581.6 8.0 %collective-permute-start.47 = (bf16[1,1,1,1,96,640]{5,4,3,2,1,0:T(8,128)(2,1)S(1)}, bf16[1,1,1,1,96,640]{5,4,3,2,1,0:T(8,128)(2,1)S(1)}, u32[]{:S(2)}, u32[]{:S(2)}) collective-permute-start(bf16[1,1,1,1,96,640]{5,4,3,2,1,0:T(8,128)(2,1)S(1)} %broadcast_select_fusion.50), channel_id=1, source_target_pairs={{0,4},{1,5},{2,6},{3,7},{4,0},{5,1},{6,2},{7,3},{8,12},{9,13},{10,... | collective-permute-start | bytes 368648 | tf_op jit(solution)/shard_map/ppermute | solution.py:225
  589.8 3.6 collective-permute-start.50
  590.8 11.9 %collective-permute-start.41 = (bf16[1,2,2,2,40,640]{5,4,3,2,1,0:T(8,128)(2,1)S(1)}, bf16[1,2,2,2,40,640]{5,4,3,2,1,0:T(8,128)(2,1)S(1)}, u32[]{:S(2)}, u32[]{:S(2)}) collective-permute-start(bf16[1,2,2,2,40,640]{5,4,3,2,1,0:T(8,128)(2,1)S(1)} %bitcast.430), channel_id=1, source_target_pairs={{0,8},{8,0},{1,9},{9,1},{2,10},{10,2},{3,11},{11,3},{4,12},{12,4},... | collective-permute-start | bytes 1228808 | tf_op jit(solution)/shard_map/ppermute | solution.py:222
  592.4 13.9 %collective-permute-start.37 = (bf16[2,2,2,1,48,640]{5,4,3,2,1,0:T(8,128)(2,1)S(1)}, bf16[2,2,2,1,48,640]{5,4,3,2,1,0:T(8,128)(2,1)S(1)}, u32[]{:S(2)}, u32[]{:S(2)}) collective-permute-start(bf16[2,2,2,1,48,640]{5,4,3,2,1,0:T(8,128)(2,1)S(1)} %broadcast_select_fusion.18), channel_id=1, source_target_pairs={{0,1},{1,0},{2,3},{3,2},{4,5},{5,4},{6,7},{7,6},{8,9},{9,8},{10,11... | collective-permute-start | bytes 1474568 | tf_op jit(solution)/shard_map/ppermute | solution.py:225
  602.9 7.3 %collective-permute-start.42 = (bf16[1,2,2,1,40,640]{5,4,3,2,1,0:T(8,128)(2,1)S(1)}, bf16[1,2,2,1,40,640]{5,4,3,2,1,0:T(8,128)(2,1)S(1)}, u32[]{:S(2)}, u32[]{:S(2)}) collective-permute-start(bf16[1,2,2,1,40,640]{5,4,3,2,1,0:T(8,128)(2,1)S(1)} %broadcast_select_fusion.45), channel_id=1, source_target_pairs={{0,1},{1,0},{2,3},{3,2},{4,5},{5,4},{6,7},{7,6},{8,9},{9,8},{10,11... | collective-permute-start | bytes 614408 | tf_op jit(solution)/shard_map/ppermute | solution.py:225
  606.4 8.6 %collective-permute-start.38 = (bf16[1,2,2,1,48,640]{5,4,3,2,1,0:T(8,128)(2,1)S(1)}, bf16[1,2,2,1,48,640]{5,4,3,2,1,0:T(8,128)(2,1)S(1)}, u32[]{:S(2)}, u32[]{:S(2)}) collective-permute-start(bf16[1,2,2,1,48,640]{5,4,3,2,1,0:T(8,128)(2,1)S(1)} %broadcast_select_fusion.28), channel_id=1, source_target_pairs={{0,8},{8,0},{1,9},{9,1},{2,10},{10,2},{3,11},{11,3},{4,12},{12,4},... | collective-permute-start | bytes 737288 | tf_op jit(solution)/shard_map/ppermute | solution.py:222
  610.2 4.7 collective-permute-start.43
  615.1 5.5 collective-permute-start.39
  615.2 5.6 collective-permute-start.44
  620.6 5.2 collective-permute-start.40
  625.9 1.4 collective-permute-start.45
  (168 other events, 770.5 us)
Sparse Core Ops, SparseCore 0:
  11.3 95.3 all-gather.8
  194.2 47.3 all-gather.4
  267.1 44.2 all-gather.6
  350.7 69.2 reduce-scatter.2
  483.4 72.9 reduce-scatter.4

commit v3 on v2

--- a/solution.py
+++ b/solution.py
@@ -109,8 +109,8 @@
     return own.reshape(micro_count, row_count, 2 * HEAD_DIM).astype(jnp.float32)
 
 
-def forward_layer(inputs, weights, tables, visible):
-    w_qkv, w_out, w_gate_up, w_down, gains = weights
+def forward_layer(inputs, first_weights, tables, visible, late_weights):
+    w_qkv, w_out, gains = first_weights
     micro_count, row_count = tables[0].shape[:2]
     normed = rms_scale(inputs, gains[:D]).astype(jnp.bfloat16)
     projected = contract_cols(normed, w_qkv)
@@ -118,6 +118,7 @@
         projected, gains[4 * D : 4 * D + HEAD_DIM], gains[4 * D + HEAD_DIM :], tables
     )
     packed = jnp.concatenate([key_rows, value_rows], axis=-1).astype(jnp.bfloat16)
+    packed, chains = late_weights.begin(packed)
     keys = gather_keys(packed)
     queries = queries.astype(jnp.bfloat16).reshape(micro_count, HEADS * row_count, HEAD_DIM)
     scores = by_micro("mqd,mkd->mqk", queries, keys[..., :HEAD_DIM]) * HEAD_DIM ** (-0.5)
@@ -130,6 +131,7 @@
     attended = side_by_side(
         gathered.reshape(micro_count, HEADS, row_count, HEAD_DIM).astype(jnp.bfloat16)
     )
+    attended, w_gate_up, w_down = late_weights.end(attended, chains)
     branch = jnp.dot(attended, w_out, preferred_element_type=jnp.float32)
     hidden = inputs + rms_scale(branch, gains[D : 2 * D])
     normed_ffw = rms_scale(hidden, gains[2 * D : 3 * D]).astype(jnp.bfloat16)
@@ -141,7 +143,7 @@
         inputs, normed, projected, queries, keys, probability, gathered, attended,
         branch, hidden, normed_ffw, gate_up, activated, branch_ffw,
     )
-    return (output, kept)
+    return (output, kept, (w_qkv, w_out, w_gate_up, w_down, gains))
 
 
 def backward_layer(incoming, kept, weights, tables, leading, pending):
@@ -165,13 +167,13 @@
     unused, pullback = jax.vjp(rms_scale, hidden, gains[2 * D : 3 * D])
     grad_hidden, gain_pre_ffw = pullback(grad_normed_ffw)
     grad_hidden = grad_hidden + incoming
-    own_chains = start_group((grad_w_gate_up, grad_w_down), leading, owners)
     if pending:
         grad_hidden, pending = held_until(grad_hidden, advance(pending, 2))
     unused, pullback = jax.vjp(rms_scale, branch, gains[D : 2 * D])
     grad_branch, gain_post_attn = pullback(grad_hidden)
     grad_branch = grad_branch.astype(jnp.bfloat16)
     grad_w_out = contract_rows(attended, grad_branch)
+    own_chains = start_group((grad_w_gate_up, grad_w_down, grad_w_out), leading, owners)
     grad_attended = contract_cols(grad_branch, w_out).astype(jnp.bfloat16)
     grad_rows = stack_heads(grad_attended, micro_count)
     grad_rows = grad_rows.reshape(micro_count, HEADS * row_count, HEAD_DIM)
@@ -209,7 +211,7 @@
     )
     gain_rows = gain_grads.reshape(owners, 1, -1)
     gain_rows = jnp.pad(gain_rows, ((0, 0), (0, GAIN_ROWS - 1), (0, D - gain_rows.shape[-1])))
-    last_chains = start_group((grad_w_qkv, grad_w_out, gain_rows), leading, owners)
+    last_chains = start_group((grad_w_qkv, gain_rows), leading, owners)
     return (grad_inputs, own_chains + last_chains, pending)
 
 
@@ -237,16 +239,35 @@
     return ([last, 0] if first else [0, last]) + inner
 
 
-def gathered_by_doubling(shard, first):
-    piece = shard.reshape((1,) * (seq_bits() + 1) + shard.shape)
-    for dim in halving_order(first)[::-1]:
-        received = across(piece, dim)
-        piece = jnp.where(
-            upper_side(dim),
-            jnp.concatenate([received, piece], axis=dim),
-            jnp.concatenate([piece, received], axis=dim),
-        )
-    return piece.reshape((-1,) + shard.shape)
+def start_doubling(shard):
+    half = shard.shape[0] // 2
+    ones = (1,) * (seq_bits() + 1)
+    return [
+        (piece.reshape(ones + piece.shape), halving_order(first)[::-1])
+        for piece, first in ((shard[:half], True), (shard[half:], False))
+    ]
+
+
+def double(chains, count):
+    moved = []
+    for piece, order in chains:
+        for dim in order[:count]:
+            received = across(piece, dim)
+            piece = jnp.where(
+                upper_side(dim),
+                jnp.concatenate([received, piece], axis=dim),
+                jnp.concatenate([piece, received], axis=dim),
+            )
+        moved.append((piece, order[count:]))
+    return moved
+
+
+def doubled(chains):
+    pieces = [piece for piece, order in double(chains, seq_bits() + 1)]
+    pieces = [piece.reshape((-1,) + piece.shape[-2:]) for piece in pieces]
+    own = jnp.concatenate(pieces, axis=1)
+    other = jnp.concatenate([swapped(piece) for piece in pieces], axis=1)
+    return (own, other)
 
 
 def advance(chains, count):
@@ -270,6 +291,22 @@
 def held_until(array, chains):
     tied = lax.optimization_barrier((array,) + tuple(total for total, order in chains))
     return (tied[0], [(total, chain[1]) for total, chain in zip(tied[1:], chains)])
+
+
+def start_group(grads, leading, owners):
+    pieces = jnp.concatenate(
+        [g.astype(jnp.bfloat16).reshape(owners, -1, D) for g in grads], axis=1
+    )
+    half = pieces.shape[1] // 2
+    front, back = pieces[:, :half], pieces[:, half:]
+    received = swapped(jnp.where(leading, back, front))
+    summed = jnp.where(leading, front, back) + received
+    cut = -(-half // 32) * 16 if half > 32 else half // 2
+    sizes = (2,) * (seq_bits() + 1)
+    return [
+        (piece.reshape(sizes + piece.shape[1:]), halving_order(first))
+        for piece, first in ((summed[:, :cut], True), (summed[:, cut:], False))
+    ]
 
 
 def start_group(grads, leading, owners):
@@ -330,18 +367,43 @@
     gain_block = jnp.pad(gains, ((0, GAIN_ROWS - 1), (0, D - gain_count)))
     early = jnp.concatenate([w_qkv[0].T, w_out[0], gain_block], axis=0)
     late = jnp.concatenate([w_gate_up[0].T, w_down[0]], axis=0)
-    early = both_layers(early)
-    late = both_layers_by_doubling(late)
-
-    def layer_weights(layer):
+    early_chains = double(start_doubling(early), 2)
+    late, early_chains = held_until(late, early_chains)
+    early = doubled(early_chains)
+    late_chains = start_doubling(late)
+
+    def first_weights(layer):
         own_gains = rows_of(early, layer, leading, qkv_rows + out_rows, 1)
         return (
             rows_of(early, layer, leading, 0, qkv_rows),
             rows_of(early, layer, leading, qkv_rows, out_rows),
-            rows_of(late, layer, leading, 0, gate_up_rows),
-            rows_of(late, layer, leading, gate_up_rows, down_rows),
             own_gains[:, :gain_count].reshape(-1).astype(jnp.float32),
         )
+
+    def late_pieces(pair, layer):
+        return (
+            rows_of(pair, layer, leading, 0, gate_up_rows),
+            rows_of(pair, layer, leading, gate_up_rows, down_rows),
+        )
+
+    arrived = []
+
+    class LowerLate:
+        def begin(packed):
+            return held_until(packed, double(late_chains, 2))
+
+        def end(array, chains):
+            own, other = doubled(chains)
+            array, own, other = lax.optimization_barrier((array, own, other))
+            arrived.append((own, other))
+            return (array,) + late_pieces((own, other), 0)
+
+    class UpperLate:
+        def begin(packed):
+            return (packed, None)
+
+        def end(array, chains):
+            return (array,) + late_pieces(arrived[0], 1)
 
     feeds = section_feeds[0, :, 0]
     micro_count, shard_rows = feeds.shape[:2]
@@ -362,16 +424,18 @@
     query_index = jnp.tile(query_index, HEADS)
     query_place = jnp.tile(position, (1, HEADS))
 
-    lower = layer_weights(0)
-    upper = layer_weights(1)
     tables = (angle_tables(position, 1000000.0), angle_tables(position, 10000.0))
     visible = (
         visibility(query_index, query_place, key_index, None),
         visibility(query_index, query_place, key_index, WINDOW),
     )
-    middle, kept_lower = forward_layer(first_in.astype(jnp.float32), lower, tables[0], visible[0])
+    middle, kept_lower, lower = forward_layer(
+        first_in.astype(jnp.float32), first_weights(0), tables[0], visible[0], LowerLate
+    )
     middle = middle.astype(jnp.bfloat16).astype(jnp.float32)
-    output, kept_upper = forward_layer(middle, upper, tables[1], visible[1])
+    output, kept_upper, upper = forward_layer(
+        middle, first_weights(1), tables[1], visible[1], UpperLate
+    )
     output = output.astype(jnp.bfloat16)
 
     grad_middle, upper_chains, unused = backward_layer(
@@ -396,10 +460,10 @@
     return (
         section_end[None, :, None],
         early_grads[:qkv_rows].T[None],
-        early_grads[qkv_rows : qkv_rows + out_rows][None],
+        late_grads[gate_up_rows + down_rows :][None],
         late_grads[:gate_up_rows].T[None],
-        late_grads[gate_up_rows:][None],
-        early_grads[qkv_rows + out_rows, :gain_count][None],
+        late_grads[gate_up_rows : gate_up_rows + down_rows][None],
+        early_grads[qkv_rows, :gain_count][None],
     )
 
 

time: 642 us -> 697 us (1.086)
  other arithmetic: 99.9 us -> 153 us
  waiting for transfers between devices: 366 us -> 316 us
  local copies, waits for them, and re-layouts: 42.7 us -> 83 us
  starting transfers between devices: 46 us -> 58.3 us
    ppermute x30 -> x36, waiting for transfers between devices: 134 us -> 193 us  [across(): return lax.ppermute(array, 'seq', [(i, i ^ step) for i in range(size)])]
    all_gather x1 -> x0, waiting for transfers between devices: 45.7 us -> none  [both_layers(): own = lax.all_gather(shard, ('dp', 'seq'), axis=0)]
    reduce_scatter x2, waiting for transfers between devices: 39.7 us -> 0.47 us  [scatter_keys(): lax.psum_scatter(pieces, ('pipe', 'seq'), scatter_dimension=0, tiled=True)]
    all_gather x2, waiting for transfers between devices: 67 us -> 43.7 us  [gather_keys(): everyone = lax.all_gather(packed, ('pipe', 'seq'), axis=0)]
    ppermute x0 -> x8, local copies, waits for them, and re-layouts: none -> 17 us  [the longest x4 9.32 us: across(): return lax.ppermute(array, 'dp', [(0, 1), (1, 0)])]
    select_n x8 -> x16, other arithmetic: 16 us -> 32.9 us  [double(): jnp.where(upper_side(dim), jnp.concatenate([received, piece], axis=dim),...]
    concatenate x5 -> x8, other arithmetic: 2.22 us -> 16.6 us  [the longest x1 7.83 us: doubled(): own = jnp.concatenate(pieces, axis=1)]
    select_n x2 -> x8, local copies, waits for them, and re-layouts: 3.26 us -> 15.1 us  [the longest x6 10.2 us: advance(): received = across(jnp.where(high, low_half, high_half), dim)]
  transfers between devices with their start and end apart: 56 -> 64, of which waited for: 31 -> 40; matrix products, arithmetic and copies ran while one was open for 19% -> 27% of each run, Pallas kernels for 0% -> 0%
where the time goes in v3:
time: 697 us; the launch traced here: 689 us
  waiting for transfers between devices  316 us (45%)
  other arithmetic  153 us (22%)
  local copies, waits for them, and re-layouts  83 us (12%)
  matrix products  61 us (9%)
  starting transfers between devices  58.3 us (8%)
  between operations  17.3 us (2%)
    ppermute x36, waiting for transfers between devices, across(): return lax.ppermute(array, 'seq', [(i, i ^ step) for i in range(size)])  193 us
    ppermute x12, waiting for transfers between devices, across(): return lax.ppermute(array, 'dp', [(0, 1), (1, 0)])  78.6 us
    all_gather x2, waiting for transfers between devices, gather_keys(): everyone = lax.all_gather(packed, ('pipe', 'seq'), axis=0)  43.7 us
    ppermute x36, starting transfers between devices, across(): return lax.ppermute(array, 'seq', [(i, i ^ step) for i in range(size)])  40.1 us
    select_n x16, other arithmetic, double(): jnp.where(upper_side(dim), jnp.concatenate([received, piece], axis=dim),...  32.9 us
    unnamed x374, local copies, waits for them, and re-layouts  22.3 us
    select_n x5, other arithmetic, rows_of(): jnp.where(first, own[:, begin:begin + count], other[:, begin:begin + count])  20.7 us
    add x28, other arithmetic, advance(): total = jnp.where(high, high_half, low_half) + received  18.3 us
  transfers between devices with their start and end apart: 64, of which 40 were waited for; matrix products, arithmetic and copies ran while one was open for 27% of the time, Pallas kernels for 0%

profile of v3, /device:TPU:0, one launch (start us, length us, event | category | flops | bytes accessed | tf_op | source)
XLA Modules:
  0.0 688.5 jit_solution(7780636602999163416)
XLA Ops:
  8.2 4.1 collective-permute-start.1
  14.6 6.5 collective-permute-done.1
  23.7 6.0 collective-permute-done.2
  29.8 2.5 collective-permute-done.4
  34.1 8.7 %collective-permute-done.5 = bf16[1,2,2,1,88,640]{5,4,3,2,1,0:T(8,128)(2,1)} collective-permute-done((bf16[1,2,2,1,88,640]{5,4,3,2,1,0:T(8,128)(2,1)S(1)}, bf16[1,2,2,1,88,640]{5,4,3,2,1,0:T(8,128)(2,1)}, u32[]{:S(2)}, u32[]{:S(2)}) %collective-permute-start.5) | collective-permute-done | bytes 450592 | tf_op jit(solution)/shard_map/ppermute | solution.py:227
  46.5 26.4 %collective-permute-done.8 = bf16[1,2,2,1,88,640]{5,4,3,2,1,0:T(8,128)(2,1)} collective-permute-done((bf16[1,2,2,1,88,640]{5,4,3,2,1,0:T(8,128)(2,1)S(1)}, bf16[1,2,2,1,88,640]{5,4,3,2,1,0:T(8,128)(2,1)}, u32[]{:S(2)}, u32[]{:S(2)}) %collective-permute-start.8) | collective-permute-done | bytes 450592 | tf_op jit(solution)/shard_map/ppermute | solution.py:224
  79.0 6.1 collective-permute-start.11
  86.4 16.3 %collective-permute-done.11 = bf16[1,1,1,1,192,640]{5,4,3,2,1,0:T(8,128)(2,1)S(1)} collective-permute-done((bf16[1,1,1,1,192,640]{5,4,3,2,1,0:T(8,128)(2,1)}, bf16[1,1,1,1,192,640]{5,4,3,2,1,0:T(8,128)(2,1)S(1)}, u32[]{:S(2)}, u32[]{:S(2)}) %collective-permute-start.11) | collective-permute-done | bytes 245792 | tf_op jit(solution)/shard_map/ppermute | solution.py:227
  104.7 3.2 collective-permute-done.13
  109.5 3.1 maximum_select_fusion.5
  112.9 5.5 collective-permute-done.12
  119.6 9.3 %collective-permute-done.14 = bf16[1,2,1,1,192,640]{5,4,3,2,1,0:T(8,128)(2,1)S(1)} collective-permute-done((bf16[1,2,1,1,192,640]{5,4,3,2,1,0:T(8,128)(2,1)S(1)}, bf16[1,2,1,1,192,640]{5,4,3,2,1,0:T(8,128)(2,1)S(1)}, u32[]{:S(2)}, u32[]{:S(2)}) %collective-permute-start.14) | collective-permute-done | bytes 491552 | tf_op jit(solution)/shard_map/ppermute | solution.py:227
  131.3 3.5 broadcast_select_fusion.6
  139.7 24.0 %collective-permute-done.17 = bf16[1,2,2,1,192,640]{5,4,3,2,1,0:T(8,128)(2,1)} collective-permute-done((bf16[1,2,2,1,192,640]{5,4,3,2,1,0:T(8,128)(2,1)}, bf16[1,2,2,1,192,640]{5,4,3,2,1,0:T(8,128)(2,1)}, u32[]{:S(2)}, u32[]{:S(2)}) %collective-permute-start.17) | collective-permute-done | bytes 983072 | tf_op jit(solution)/shard_map/ppermute | solution.py:227
  163.6 3.9 maximum_select_fusion.3
  169.1 3.3 maximum_select_fusion.2
  174.5 37.4 %collective-permute-done.18 = bf16[1,2,2,2,192,640]{5,4,3,2,1,0:T(8,128)(2,1)} collective-permute-done((bf16[1,2,2,2,192,640]{5,4,3,2,1,0:T(8,128)(2,1)}, bf16[1,2,2,2,192,640]{5,4,3,2,1,0:T(8,128)(2,1)}, u32[]{:S(2)}, u32[]{:S(2)}) %collective-permute-start.18) | collective-permute-done | bytes 1966112 | tf_op jit(solution)/shard_map/ppermute | solution.py:224
  211.8 5.7 maximum_select_fusion.1
  217.5 2.5 collective-permute-done.16
  220.0 6.3 maximum_select_fusion
  229.8 2.7 broadcast_select_fusion.10
  232.5 7.8 %pad_maximum_fusion = bf16[16,384,640]{2,1,0:T(8,128)(2,1)} fusion(bf16[16,192,640]{2,1,0:T(8,128)(2,1)} %bitcast.47, bf16[16,192,640]{2,1,0:T(8,128)(2,1)} %bitcast.46), kind=kLoop, calls=%fused_computation.2 | loop fusion | flops 15728640 | bytes 15728640 | tf_op jit(solution)/shard_map/concatenate | solution.py:268
  240.3 4.1 copy.82
  244.4 5.3 fusion.175
  249.8 3.9 fusion.176
  253.8 7.5 %pad_maximum_fusion.1 = bf16[16,384,640]{2,1,0:T(8,128)(2,1)} fusion(bf16[16,192,640]{2,1,0:T(8,128)(2,1)} %collective-permute-done.20, bf16[16,192,640]{2,1,0:T(8,128)(2,1)} %collective-permute-done.19), kind=kLoop, calls=%fused_computation.3 | loop fusion | flops 15728640 | bytes 15728640 | tf_op jit(solution)/shard_map/concatenate | solution.py:269
  261.2 8.9 %broadcast_select_fusion = (bf16[16,256,640]{2,1,0:T(8,128)(2,1)}, bf16[16,256,640]{2,1,0:T(8,128)(2,1)}) fusion(pred[]{:T(512)S(6)} %not.2, bf16[16,384,640]{2,1,0:T(8,128)(2,1)} %pad_maximum_fusion.1, bf16[16,384,640]{2,1,0:T(8,128)(2,1)} %pad_maximum_fusion, pred[]{:T(512)S(6)} %eq.10), kind=kLoop, calls=%fused_computation.6 | loop fusion | flops 5242880 | bytes 20971522 | tf_op jit(solution)/shard_map/jit(_where)/select_n | solution.py:344
  270.1 4.7 broadcast_select_fusion.4
  286.0 43.7 %all-gather.4.cloned.1.call-done = bf16[16,3,64,512]{3,2,1,0:T(8,128)(2,1)} async-done(((bf16[1,3,64,512]{3,2,1,0:T(8,128)(2,1)}), bf16[16,3,64,512]{3,2,1,0:T(8,128)(2,1)}) %all-gather.4.cloned.1.call-update) | async-done | bytes 3145744 | tf_op jit(solution)/shard_map/all_gather | solution.py:99
  329.7 4.1 copy.85
  333.8 6.2 fusion.177
  340.0 3.1 fusion.178
  359.1 3.0 broadcast_select_fusion.3
  369.9 2.6 fusion.47
  373.3 5.6 select_add_fusion.1
  382.7 3.2 copy.94
  391.3 3.3 broadcast_select_fusion.16
  398.0 2.4 copy.99
  400.5 25.2 %collective-permute-done.22 = bf16[2,2,2,1,112,640]{5,4,3,2,1,0:T(8,128)(2,1)} collective-permute-done((bf16[2,2,2,1,112,640]{5,4,3,2,1,0:T(8,128)(2,1)}, bf16[2,2,2,1,112,640]{5,4,3,2,1,0:T(8,128)(2,1)}, u32[]{:S(2)}, u32[]{:S(2)}) %collective-permute-start.22) | collective-permute-done | bytes 1146912 | tf_op jit(solution)/shard_map/ppermute | solution.py:227
  443.7 2.9 collective-permute-done.23
  450.9 4.2 collective-permute-done.25
  464.9 2.8 multiply_reduce_fusion.8
  467.7 4.2 convolution_convert_fusion
  480.1 4.7 collective-permute-done.26
  488.1 3.3 collective-permute-done.28
  498.2 3.2 collective-permute-done.29
  508.2 2.7 collective-permute-done.32
  512.0 3.2 broadcast_select_fusion.2
  524.7 2.6 fusion.44
  530.9 3.9 select_add_fusion
  538.5 3.2 copy.114
  542.9 2.4 copy.115
  546.8 3.2 broadcast_select_fusion.14
  558.7 21.0 %collective-permute-done.36 = bf16[2,2,2,1,112,640]{5,4,3,2,1,0:T(8,128)(2,1)} collective-permute-done((bf16[2,2,2,1,112,640]{5,4,3,2,1,0:T(8,128)(2,1)}, bf16[2,2,2,1,112,640]{5,4,3,2,1,0:T(8,128)(2,1)}, u32[]{:S(2)}, u32[]{:S(2)}) %collective-permute-start.36) | collective-permute-done | bytes 1146912 | tf_op jit(solution)/shard_map/ppermute | solution.py:227
  579.7 2.5 copy.116
  588.3 2.6 copy.120
  602.7 3.7 collective-permute-done.39
  618.0 7.8 %collective-permute-done.57 = bf16[1,2,1,1,112,640]{4,5,3,2,1,0:T(8,128)(2,1)S(1)} collective-permute-done((bf16[1,2,1,1,112,640]{4,5,3,2,1,0:T(8,128)(2,1)S(1)}, bf16[1,2,1,1,112,640]{4,5,3,2,1,0:T(8,128)(2,1)S(1)}, u32[]{:S(2)}, u32[]{:S(2)}) %collective-permute-start.57) | collective-permute-done | bytes 286752 | tf_op jit(solution)/shard_map/ppermute | solution.py:227
  627.0 8.9 %collective-permute-done.55 = bf16[1,2,1,1,112,640]{4,5,3,2,1,0:T(8,128)(2,1)S(1)} collective-permute-done((bf16[1,2,1,1,112,640]{4,5,3,2,1,0:T(8,128)(2,1)S(1)}, bf16[1,2,1,1,112,640]{4,5,3,2,1,0:T(8,128)(2,1)S(1)}, u32[]{:S(2)}, u32[]{:S(2)}) %collective-permute-start.55) | collective-permute-done | bytes 286752 | tf_op jit(solution)/shard_map/ppermute | solution.py:227
  636.3 9.5 %collective-permute-done.56 = bf16[1,1,1,1,112,640]{4,5,3,2,1,0:T(8,128)(2,1)S(1)} collective-permute-done((bf16[1,1,1,1,112,640]{4,5,3,2,1,0:T(8,128)(2,1)S(1)}, bf16[1,1,1,1,112,640]{4,5,3,2,1,0:T(8,128)(2,1)S(1)}, u32[]{:S(2)}, u32[]{:S(2)}) %collective-permute-start.56) | collective-permute-done | bytes 143392 | tf_op jit(solution)/shard_map/ppermute | solution.py:227
  652.0 6.6 collective-permute-done.50
  660.6 3.1 collective-permute-done.51
  665.0 3.0 collective-permute-done.52
  673.8 2.8 collective-permute-start.49
  (759 shorter events, 221.9 us)
Async XLA Ops:
  7.2 233.1 %all-gather.6.cloned.1.call-start = ((), (), s32[]{:S(2)}) async-start(), calls=%async_computation.5 | async-start | bytes 3342336 | tf_op jit(solution)/shard_map/all_gather | solution.py:99
  8.2 12.9 %collective-permute-start.1 = (bf16[1,1,1,1,88,640]{5,4,3,2,1,0:T(8,128)(2,1)S(1)}, bf16[1,1,1,1,88,640]{5,4,3,2,1,0:T(8,128)(2,1)S(1)}, u32[]{:S(2)}, u32[]{:S(2)}) collective-permute-start(bf16[1,1,1,1,88,640]{5,4,3,2,1,0:T(8,128)(2,1)S(1)} %get-tuple-element.192), channel_id=1, source_target_pairs={{0,4},{1,5},{2,6},{3,7},{4,0},{5,1},{6,2},{7,3},{8,12},{9,13},{10,... | collective-permute-start | bytes 337928 | tf_op jit(solution)/shard_map/ppermute | solution.py:227
  12.3 10.4 %collective-permute-start.3 = (bf16[1,1,1,1,88,640]{5,4,3,2,1,0:T(8,128)(2,1)S(1)}, bf16[1,1,1,1,88,640]{5,4,3,2,1,0:T(8,128)(2,1)S(1)}, u32[]{:S(2)}, u32[]{:S(2)}) collective-permute-start(bf16[1,1,1,1,88,640]{5,4,3,2,1,0:T(8,128)(2,1)S(1)} %get-tuple-element.185), channel_id=1, source_target_pairs={{0,4},{1,5},{2,6},{3,7},{4,0},{5,1},{6,2},{7,3},{8,12},{9,13},{10,... | collective-permute-start | bytes 337928 | tf_op jit(solution)/shard_map/ppermute | solution.py:227
  21.2 8.5 %collective-permute-start.2 = (bf16[1,2,1,1,88,640]{5,4,3,2,1,0:T(8,128)(2,1)S(1)}, bf16[1,2,1,1,88,640]{5,4,3,2,1,0:T(8,128)(2,1)S(1)}, u32[]{:S(2)}, u32[]{:S(2)}) collective-permute-start(bf16[1,2,1,1,88,640]{5,4,3,2,1,0:T(8,128)(2,1)S(1)} %maximum_select_fusion.16), channel_id=1, source_target_pairs={{0,2},{1,3},{2,0},{3,1},{4,6},{5,7},{6,4},{7,5},{8,10},{9,11},{10,... | collective-permute-start | bytes 675848 | tf_op jit(solution)/shard_map/ppermute | solution.py:227
  22.8 9.5 %collective-permute-start.4 = (bf16[1,2,1,1,88,640]{5,4,3,2,1,0:T(8,128)(2,1)S(1)}, bf16[1,2,1,1,88,640]{5,4,3,2,1,0:T(8,128)(2,1)S(1)}, u32[]{:S(2)}, u32[]{:S(2)}) collective-permute-start(bf16[1,2,1,1,88,640]{5,4,3,2,1,0:T(8,128)(2,1)S(1)} %maximum_select_fusion.18), channel_id=1, source_target_pairs={{0,2},{1,3},{2,0},{3,1},{4,6},{5,7},{6,4},{7,5},{8,10},{9,11},{10,... | collective-permute-start | bytes 675848 | tf_op jit(solution)/shard_map/ppermute | solution.py:227
  32.5 10.4 %collective-permute-start.5 = (bf16[1,2,2,1,88,640]{5,4,3,2,1,0:T(8,128)(2,1)S(1)}, bf16[1,2,2,1,88,640]{5,4,3,2,1,0:T(8,128)(2,1)}, u32[]{:S(2)}, u32[]{:S(2)}) collective-permute-start(bf16[1,2,2,1,88,640]{5,4,3,2,1,0:T(8,128)(2,1)S(1)} %maximum_select_fusion.15), channel_id=1, source_target_pairs={{0,1},{1,0},{2,3},{3,2},{4,5},{5,4},{6,7},{7,6},{8,9},{9,8},{10,11... | collective-permute-start | bytes 1351688 | tf_op jit(solution)/shard_map/ppermute | solution.py:227
  44.2 31.4 %collective-permute-start.6 = (bf16[1,2,2,2,88,640]{5,4,3,2,1,0:T(8,128)(2,1)S(1)}, bf16[1,2,2,2,88,640]{5,4,3,2,1,0:T(8,128)(2,1)}, u32[]{:S(2)}, u32[]{:S(2)}) collective-permute-start(bf16[1,2,2,2,88,640]{5,4,3,2,1,0:T(8,128)(2,1)S(1)} %maximum_select_fusion.8), channel_id=1, source_target_pairs={{0,8},{8,0},{1,9},{9,1},{2,10},{10,2},{3,11},{11,3},{4,12},{12,4},... | collective-permute-start | bytes 2703368 | tf_op jit(solution)/shard_map/ppermute | solution.py:224
  45.5 27.4 %collective-permute-start.8 = (bf16[1,2,2,1,88,640]{5,4,3,2,1,0:T(8,128)(2,1)S(1)}, bf16[1,2,2,1,88,640]{5,4,3,2,1,0:T(8,128)(2,1)}, u32[]{:S(2)}, u32[]{:S(2)}) collective-permute-start(bf16[1,2,2,1,88,640]{5,4,3,2,1,0:T(8,128)(2,1)S(1)} %maximum_select_fusion.14), channel_id=1, source_target_pairs={{0,8},{8,0},{1,9},{9,1},{2,10},{10,2},{3,11},{11,3},{4,12},{12,4},... | collective-permute-start | bytes 1351688 | tf_op jit(solution)/shard_map/ppermute | solution.py:224
  46.3 39.0 %collective-permute-start = (bf16[3,64,640]{2,1,0:T(8,128)(2,1)S(1)}, bf16[3,64,640]{2,1,0:T(8,128)(2,1)}, u32[]{:S(2)}, u32[]{:S(2)}) collective-permute-start(bf16[3,64,640]{2,1,0:T(8,128)(2,1)S(1)} %broadcast_select_fusion.42), channel_id=1, source_target_pairs={{0,16},{16,0},{1,17},{17,1},{2,18},{18,2},{3,19},{19,3},{4,20},{20... | collective-permute-start | bytes 737288 | tf_op jit(solution)/shard_map/ppermute | solution.py:40
  74.5 35.0 %collective-permute-start.9 = (bf16[2,2,2,1,88,640]{5,4,3,2,1,0:T(8,128)(2,1)S(1)}, bf16[2,2,2,1,88,640]{5,4,3,2,1,0:T(8,128)(2,1)}, u32[]{:S(2)}, u32[]{:S(2)}) collective-permute-start(bf16[2,2,2,1,88,640]{5,4,3,2,1,0:T(8,128)(2,1)S(1)} %maximum_select_fusion.9), channel_id=1, source_target_pairs={{0,1},{1,0},{2,3},{3,2},{4,5},{5,4},{6,7},{7,6},{8,9},{9,8},{10,11... | collective-permute-start | bytes 2703368 | tf_op jit(solution)/shard_map/ppermute | solution.py:227
  78.0 52.1 %collective-permute-start.7 = (bf16[16,88,640]{2,1,0:T(8,128)(2,1)S(1)}, bf16[16,88,640]{2,1,0:T(8,128)(2,1)}, u32[]{:S(2)}, u32[]{:S(2)}) collective-permute-start(bf16[16,88,640]{2,1,0:T(8,128)(2,1)S(1)} %bitcast.276), channel_id=1, source_target_pairs={{0,16},{16,0},{1,17},{17,1},{2,18},{18,2},{3,19},{19,3},{4,20},{20... | collective-permute-start | bytes 5406728 | tf_op jit(solution)/shard_map/ppermute | solution.py:40
  79.0 23.7 %collective-permute-start.11 = (bf16[1,1,1,1,192,640]{5,4,3,2,1,0:T(8,128)(2,1)}, bf16[1,1,1,1,192,640]{5,4,3,2,1,0:T(8,128)(2,1)S(1)}, u32[]{:S(2)}, u32[]{:S(2)}) collective-permute-start(bf16[1,1,1,1,192,640]{5,4,3,2,1,0:T(8,128)(2,1)} %get-tuple-element.162), channel_id=1, source_target_pairs={{0,4},{1,5},{2,6},{3,7},{4,0},{5,1},{6,2},{7,3},{8,12},{9,13},{10,... | collective-permute-start | bytes 737288 | tf_op jit(solution)/shard_map/ppermute | solution.py:227
  85.2 22.7 %collective-permute-start.13 = (bf16[1,1,1,1,192,640]{5,4,3,2,1,0:T(8,128)(2,1)}, bf16[1,1,1,1,192,640]{5,4,3,2,1,0:T(8,128)(2,1)S(1)}, u32[]{:S(2)}, u32[]{:S(2)}) collective-permute-start(bf16[1,1,1,1,192,640]{5,4,3,2,1,0:T(8,128)(2,1)} %get-tuple-element.159), channel_id=1, source_target_pairs={{0,4},{1,5},{2,6},{3,7},{4,0},{5,1},{6,2},{7,3},{8,12},{9,13},{10,... | collective-permute-start | bytes 737288 | tf_op jit(solution)/shard_map/ppermute | solution.py:227
  104.0 14.4 %collective-permute-start.12 = (bf16[1,2,1,1,192,640]{5,4,3,2,1,0:T(8,128)(2,1)S(1)}, bf16[1,2,1,1,192,640]{5,4,3,2,1,0:T(8,128)(2,1)S(1)}, u32[]{:S(2)}, u32[]{:S(2)}) collective-permute-start(bf16[1,2,1,1,192,640]{5,4,3,2,1,0:T(8,128)(2,1)S(1)} %maximum_select_fusion.10), channel_id=1, source_target_pairs={{0,2},{1,3},{2,0},{3,1},{4,6},{5,7},{6,4},{7,5},{8,10},{9,11},{10,... | collective-permute-start | bytes 1474568 | tf_op jit(solution)/shard_map/ppermute | solution.py:227
  109.1 19.7 %collective-permute-start.14 = (bf16[1,2,1,1,192,640]{5,4,3,2,1,0:T(8,128)(2,1)S(1)}, bf16[1,2,1,1,192,640]{5,4,3,2,1,0:T(8,128)(2,1)S(1)}, u32[]{:S(2)}, u32[]{:S(2)}) collective-permute-start(bf16[1,2,1,1,192,640]{5,4,3,2,1,0:T(8,128)(2,1)S(1)} %maximum_select_fusion.12), channel_id=1, source_target_pairs={{0,2},{1,3},{2,0},{3,1},{4,6},{5,7},{6,4},{7,5},{8,10},{9,11},{10,... | collective-permute-start | bytes 1474568 | tf_op jit(solution)/shard_map/ppermute | solution.py:227
  112.7 18.6 %collective-permute-start.10 = (bf16[16,88,640]{2,1,0:T(8,128)(2,1)}, bf16[16,88,640]{2,1,0:T(8,128)(2,1)}, u32[]{:S(2)}, u32[]{:S(2)}) collective-permute-start(bf16[16,88,640]{2,1,0:T(8,128)(2,1)} %bitcast.18), channel_id=1, source_target_pairs={{0,16},{16,0},{1,17},{17,1},{2,18},{18,2},{3,19},{19,3},{4,20},{20... | collective-permute-start | bytes 5406728 | tf_op jit(solution)/shard_map/ppermute | solution.py:40
  137.5 26.1 %collective-permute-start.17 = (bf16[1,2,2,1,192,640]{5,4,3,2,1,0:T(8,128)(2,1)}, bf16[1,2,2,1,192,640]{5,4,3,2,1,0:T(8,128)(2,1)}, u32[]{:S(2)}, u32[]{:S(2)}) collective-permute-start(bf16[1,2,2,1,192,640]{5,4,3,2,1,0:T(8,128)(2,1)} %maximum_select_fusion.7), channel_id=1, source_target_pairs={{0,1},{1,0},{2,3},{3,2},{4,5},{5,4},{6,7},{7,6},{8,9},{9,8},{10,11... | collective-permute-start | bytes 2949128 | tf_op jit(solution)/shard_map/ppermute | solution.py:227
  138.1 31.1 %collective-permute-start.15 = (bf16[1,2,2,1,192,640]{5,4,3,2,1,0:T(8,128)(2,1)}, bf16[1,2,2,1,192,640]{5,4,3,2,1,0:T(8,128)(2,1)}, u32[]{:S(2)}, u32[]{:S(2)}) collective-permute-start(bf16[1,2,2,1,192,640]{5,4,3,2,1,0:T(8,128)(2,1)} %maximum_select_fusion.6), channel_id=1, source_target_pairs={{0,8},{8,0},{1,9},{9,1},{2,10},{10,2},{3,11},{11,3},{4,12},{12,4},... | collective-permute-start | bytes 2949128 | tf_op jit(solution)/shard_map/ppermute | solution.py:224
  139.6 190.1 %all-gather.4.cloned.1.call-start = ((), (), s32[]{:S(2)}) async-start(), calls=%async_computation.2 | async-start | bytes 3342336 | tf_op jit(solution)/shard_map/all_gather | solution.py:99
  167.6 44.3 %collective-permute-start.18 = (bf16[1,2,2,2,192,640]{5,4,3,2,1,0:T(8,128)(2,1)}, bf16[1,2,2,2,192,640]{5,4,3,2,1,0:T(8,128)(2,1)}, u32[]{:S(2)}, u32[]{:S(2)}) collective-permute-start(bf16[1,2,2,2,192,640]{5,4,3,2,1,0:T(8,128)(2,1)} %maximum_select_fusion.3), channel_id=1, source_target_pairs={{0,8},{8,0},{1,9},{9,1},{2,10},{10,2},{3,11},{11,3},{4,12},{12,4},... | collective-permute-start | bytes 5898248 | tf_op jit(solution)/shard_map/ppermute | solution.py:224
  172.5 47.6 %collective-permute-start.16 = (bf16[2,2,2,1,192,640]{5,4,3,2,1,0:T(8,128)(2,1)}, bf16[2,2,2,1,192,640]{5,4,3,2,1,0:T(8,128)(2,1)}, u32[]{:S(2)}, u32[]{:S(2)}) collective-permute-start(bf16[2,2,2,1,192,640]{5,4,3,2,1,0:T(8,128)(2,1)} %maximum_select_fusion.2), channel_id=1, source_target_pairs={{0,1},{1,0},{2,3},{3,2},{4,5},{5,4},{6,7},{7,6},{8,9},{9,8},{10,11... | collective-permute-start | bytes 5898248 | tf_op jit(solution)/shard_map/ppermute | solution.py:227
  217.5 36.2 %collective-permute-start.20 = (bf16[16,192,640]{2,1,0:T(8,128)(2,1)}, bf16[16,192,640]{2,1,0:T(8,128)(2,1)}, u32[]{:S(2)}, u32[]{:S(2)}) collective-permute-start(bf16[16,192,640]{2,1,0:T(8,128)(2,1)} %bitcast.47), channel_id=1, source_target_pairs={{0,16},{16,0},{1,17},{17,1},{2,18},{18,2},{3,19},{19,3},{4,20},{20... | collective-permute-start | bytes 11796488 | tf_op jit(solution)/shard_map/ppermute | solution.py:40
  226.3 27.4 %collective-permute-start.19 = (bf16[16,192,640]{2,1,0:T(8,128)(2,1)}, bf16[16,192,640]{2,1,0:T(8,128)(2,1)}, u32[]{:S(2)}, u32[]{:S(2)}) collective-permute-start(bf16[16,192,640]{2,1,0:T(8,128)(2,1)} %bitcast.46), channel_id=1, source_target_pairs={{0,16},{16,0},{1,17},{17,1},{2,18},{18,2},{3,19},{19,3},{4,20},{20... | collective-permute-start | bytes 11796488 | tf_op jit(solution)/shard_map/ppermute | solution.py:40
  284.0 158.8 %reduce-scatter.3.cloned.1.call-start = ((), (), s32[]{:S(2)}) async-start(), calls=%async_computation.3 | async-start | bytes 3342336 | tf_op jit(solution)/shard_map/reduce_scatter | solution.py:108
  362.1 11.1 %collective-permute-start.21 = (bf16[16,224,640]{2,1,0:T(8,128)(2,1)}, bf16[16,224,640]{2,1,0:T(8,128)(2,1)}, u32[]{:S(2)}, u32[]{:S(2)}) collective-permute-start(bf16[16,224,640]{2,1,0:T(8,128)(2,1)} %broadcast_select_fusion.3), channel_id=1, source_target_pairs={{0,16},{16,0},{1,17},{17,1},{2,18},{18,2},{3,19},{19,3},{4,20},{20... | collective-permute-start | bytes 13762568 | tf_op jit(solution)/shard_map/ppermute | solution.py:40
  369.1 228.1 %reduce-scatter.5.cloned.1.call-start = ((), (), s32[]{:S(2)}) async-start(), calls=%async_computation.4 | async-start | bytes 3342336 | tf_op jit(solution)/shard_map/reduce_scatter | solution.py:108
  389.5 36.1 %collective-permute-start.22 = (bf16[2,2,2,1,112,640]{5,4,3,2,1,0:T(8,128)(2,1)}, bf16[2,2,2,1,112,640]{5,4,3,2,1,0:T(8,128)(2,1)}, u32[]{:S(2)}, u32[]{:S(2)}) collective-permute-start(bf16[2,2,2,1,112,640]{5,4,3,2,1,0:T(8,128)(2,1)} %copy.95), channel_id=1, source_target_pairs={{0,1},{1,0},{2,3},{3,2},{4,5},{5,4},{6,7},{7,6},{8,9},{9,8},{10,11... | collective-permute-start | bytes 3440648 | tf_op jit(solution)/shard_map/ppermute | solution.py:227
  394.6 38.8 %collective-permute-start.24 = (bf16[1,2,2,2,112,640]{5,4,3,2,1,0:T(8,128)(2,1)}, bf16[1,2,2,2,112,640]{5,4,3,2,1,0:T(8,128)(2,1)}, u32[]{:S(2)}, u32[]{:S(2)}) collective-permute-start(bf16[1,2,2,2,112,640]{5,4,3,2,1,0:T(8,128)(2,1)} %bitcast.92), channel_id=1, source_target_pairs={{0,8},{8,0},{1,9},{9,1},{2,10},{10,2},{3,11},{11,3},{4,12},{12,4},... | collective-permute-start | bytes 3440648 | tf_op jit(solution)/shard_map/ppermute | solution.py:224
  432.0 14.6 %collective-permute-start.23 = (bf16[1,2,2,1,112,640]{5,4,3,2,1,0:T(8,128)(2,1)}, bf16[1,2,2,1,112,640]{5,4,3,2,1,0:T(8,128)(2,1)}, u32[]{:S(2)}, u32[]{:S(2)}) collective-permute-start(bf16[1,2,2,1,112,640]{5,4,3,2,1,0:T(8,128)(2,1)} %copy.97), channel_id=1, source_target_pairs={{0,8},{8,0},{1,9},{9,1},{2,10},{10,2},{3,11},{11,3},{4,12},{12,4},... | collective-permute-start | bytes 1720328 | tf_op jit(solution)/shard_map/ppermute | solution.py:224
  440.7 14.4 %collective-permute-start.25 = (bf16[1,2,2,1,112,640]{5,4,3,2,1,0:T(8,128)(2,1)}, bf16[1,2,2,1,112,640]{5,4,3,2,1,0:T(8,128)(2,1)}, u32[]{:S(2)}, u32[]{:S(2)}) collective-permute-start(bf16[1,2,2,1,112,640]{5,4,3,2,1,0:T(8,128)(2,1)} %copy.101), channel_id=1, source_target_pairs={{0,1},{1,0},{2,3},{3,2},{4,5},{5,4},{6,7},{7,6},{8,9},{9,8},{10,11... | collective-permute-start | bytes 1720328 | tf_op jit(solution)/shard_map/ppermute | solution.py:227
  473.8 11.0 %collective-permute-start.26 = (bf16[1,2,1,1,112,640]{4,5,3,2,1,0:T(8,128)(2,1)}, bf16[1,2,1,1,112,640]{4,5,3,2,1,0:T(8,128)(2,1)}, u32[]{:S(2)}, u32[]{:S(2)}) collective-permute-start(bf16[1,2,1,1,112,640]{4,5,3,2,1,0:T(8,128)(2,1)} %broadcast_select_fusion.31), channel_id=1, source_target_pairs={{0,2},{1,3},{2,0},{3,1},{4,6},{5,7},{6,4},{7,5},{8,10},{9,11},{10,... | collective-permute-start | bytes 860168 | tf_op jit(solution)/shard_map/ppermute | solution.py:227
  476.5 14.8 %collective-permute-start.28 = (bf16[1,2,1,1,112,640]{4,5,3,2,1,0:T(8,128)(2,1)}, bf16[1,2,1,1,112,640]{4,5,3,2,1,0:T(8,128)(2,1)}, u32[]{:S(2)}, u32[]{:S(2)}) collective-permute-start(bf16[1,2,1,1,112,640]{4,5,3,2,1,0:T(8,128)(2,1)} %broadcast_select_fusion.30), channel_id=1, source_target_pairs={{0,2},{1,3},{2,0},{3,1},{4,6},{5,7},{6,4},{7,5},{8,10},{9,11},{10,... | collective-permute-start | bytes 860168 | tf_op jit(solution)/shard_map/ppermute | solution.py:227
  479.8 16.4 %collective-permute-start.30 = (bf16[16,56,640]{2,1,0:T(8,128)(2,1)S(1)}, bf16[16,56,640]{2,1,0:T(8,128)(2,1)S(1)}, u32[]{:S(2)}, u32[]{:S(2)}) collective-permute-start(bf16[16,56,640]{2,1,0:T(8,128)(2,1)S(1)} %broadcast_select_fusion.13), channel_id=1, source_target_pairs={{0,16},{16,0},{1,17},{17,1},{2,18},{18,2},{3,19},{19,3},{4,20},{20... | collective-permute-start | bytes 3440648 | tf_op jit(solution)/shard_map/ppermute | solution.py:40
  485.9 10.3 %collective-permute-start.27 = (bf16[1,1,1,1,112,640]{4,5,3,2,1,0:T(8,128)(2,1)S(1)}, bf16[1,1,1,1,112,640]{4,5,3,2,1,0:T(8,128)(2,1)S(1)}, u32[]{:S(2)}, u32[]{:S(2)}) collective-permute-start(bf16[1,1,1,1,112,640]{4,5,3,2,1,0:T(8,128)(2,1)S(1)} %broadcast_select_fusion.48), channel_id=1, source_target_pairs={{0,4},{1,5},{2,6},{3,7},{4,0},{5,1},{6,2},{7,3},{8,12},{9,13},{10,... | collective-permute-start | bytes 430088 | tf_op jit(solution)/shard_map/ppermute | solution.py:227
  492.4 8.9 %collective-permute-start.29 = (bf16[1,1,1,1,112,640]{4,5,3,2,1,0:T(8,128)(2,1)S(1)}, bf16[1,1,1,1,112,640]{4,5,3,2,1,0:T(8,128)(2,1)S(1)}, u32[]{:S(2)}, u32[]{:S(2)}) collective-permute-start(bf16[1,1,1,1,112,640]{4,5,3,2,1,0:T(8,128)(2,1)S(1)} %broadcast_select_fusion.47), channel_id=1, source_target_pairs={{0,4},{1,5},{2,6},{3,7},{4,0},{5,1},{6,2},{7,3},{8,12},{9,13},{10,... | collective-permute-start | bytes 430088 | tf_op jit(solution)/shard_map/ppermute | solution.py:227
  496.8 6.3 collective-permute-start.33
  497.5 7.8 %collective-permute-start.31 = (bf16[2,2,2,1,32,640]{5,4,3,2,1,0:T(8,128)(2,1)S(1)}, bf16[2,2,2,1,32,640]{5,4,3,2,1,0:T(8,128)(2,1)S(1)}, u32[]{:S(2)}, u32[]{:S(2)}) collective-permute-start(bf16[2,2,2,1,32,640]{5,4,3,2,1,0:T(8,128)(2,1)S(1)} %broadcast_select_fusion.27), channel_id=1, source_target_pairs={{0,1},{1,0},{2,3},{3,2},{4,5},{5,4},{6,7},{7,6},{8,9},{9,8},{10,11... | collective-permute-start | bytes 983048 | tf_op jit(solution)/shard_map/ppermute | solution.py:227
  503.2 4.9 collective-permute-start.34
  505.4 5.5 collective-permute-start.32
  515.3 15.0 %collective-permute-start.35 = (bf16[16,224,640]{2,1,0:T(8,128)(2,1)}, bf16[16,224,640]{2,1,0:T(8,128)(2,1)}, u32[]{:S(2)}, u32[]{:S(2)}) collective-permute-start(bf16[16,224,640]{2,1,0:T(8,128)(2,1)} %broadcast_select_fusion.2), channel_id=1, source_target_pairs={{0,16},{16,0},{1,17},{17,1},{2,18},{18,2},{3,19},{19,3},{4,20},{20... | collective-permute-start | bytes 13762568 | tf_op jit(solution)/shard_map/ppermute | solution.py:40
  522.5 30.9 %collective-permute-start.40 = (bf16[1,2,1,1,32,640]{5,4,3,2,1,0:T(8,128)(2,1)S(1)}, bf16[1,2,1,1,32,640]{5,4,3,2,1,0:T(8,128)(2,1)S(1)}, u32[]{:S(2)}, u32[]{:S(2)}) collective-permute-start(bf16[1,2,1,1,32,640]{5,4,3,2,1,0:T(8,128)(2,1)S(1)} %broadcast_select_fusion.52), channel_id=1, source_target_pairs={{0,2},{1,3},{2,0},{3,1},{4,6},{5,7},{6,4},{7,5},{8,10},{9,11},{10,... | collective-permute-start | bytes 245768 | tf_op jit(solution)/shard_map/ppermute | solution.py:227
  523.4 22.5 %collective-permute-start.42 = (bf16[1,2,1,1,24,640]{5,4,3,2,1,0:T(8,128)(2,1)S(1)}, bf16[1,2,1,1,24,640]{5,4,3,2,1,0:T(8,128)(2,1)}, u32[]{:S(2)}, u32[]{:S(2)}) collective-permute-start(bf16[1,2,1,1,24,640]{5,4,3,2,1,0:T(8,128)(2,1)S(1)} %broadcast_select_fusion.60), channel_id=1, source_target_pairs={{0,2},{1,3},{2,0},{3,1},{4,6},{5,7},{6,4},{7,5},{8,10},{9,11},{10,... | collective-permute-start | bytes 184328 | tf_op jit(solution)/shard_map/ppermute | solution.py:227
  545.4 34.4 %collective-permute-start.36 = (bf16[2,2,2,1,112,640]{5,4,3,2,1,0:T(8,128)(2,1)}, bf16[2,2,2,1,112,640]{5,4,3,2,1,0:T(8,128)(2,1)}, u32[]{:S(2)}, u32[]{:S(2)}) collective-permute-start(bf16[2,2,2,1,112,640]{5,4,3,2,1,0:T(8,128)(2,1)} %copy.115), channel_id=1, source_target_pairs={{0,1},{1,0},{2,3},{3,2},{4,5},{5,4},{6,7},{7,6},{8,9},{9,8},{10,11... | collective-permute-start | bytes 3440648 | tf_op jit(solution)/shard_map/ppermute | solution.py:227
  550.0 38.3 %collective-permute-start.38 = (bf16[1,2,2,2,112,640]{5,4,3,2,1,0:T(8,128)(2,1)}, bf16[1,2,2,2,112,640]{5,4,3,2,1,0:T(8,128)(2,1)}, u32[]{:S(2)}, u32[]{:S(2)}) collective-permute-start(bf16[1,2,2,2,112,640]{5,4,3,2,1,0:T(8,128)(2,1)} %bitcast.124), channel_id=1, source_target_pairs={{0,8},{8,0},{1,9},{9,1},{2,10},{10,2},{3,11},{11,3},{4,12},{12,4},... | collective-permute-start | bytes 3440648 | tf_op jit(solution)/shard_map/ppermute | solution.py:224
  552.7 41.7 %collective-permute-start.43 = (bf16[1,1,1,1,24,640]{5,4,3,2,1,0:T(8,128)(2,1)}, bf16[1,1,1,1,24,640]{5,4,3,2,1,0:T(8,128)(2,1)}, u32[]{:S(2)}, u32[]{:S(2)}) collective-permute-start(bf16[1,1,1,1,24,640]{5,4,3,2,1,0:T(8,128)(2,1)} %broadcast_select_fusion.64), channel_id=1, source_target_pairs={{0,4},{1,5},{2,6},{3,7},{4,0},{5,1},{6,2},{7,3},{8,12},{9,13},{10,... | collective-permute-start | bytes 92168 | tf_op jit(solution)/shard_map/ppermute | solution.py:227
  554.1 41.7 %collective-permute-start.41 = (bf16[1,1,1,1,32,640]{5,4,3,2,1,0:T(8,128)(2,1)}, bf16[1,1,1,1,32,640]{5,4,3,2,1,0:T(8,128)(2,1)}, u32[]{:S(2)}, u32[]{:S(2)}) collective-permute-start(bf16[1,1,1,1,32,640]{5,4,3,2,1,0:T(8,128)(2,1)} %broadcast_select_fusion.62), channel_id=1, source_target_pairs={{0,4},{1,5},{2,6},{3,7},{4,0},{5,1},{6,2},{7,3},{8,12},{9,13},{10,... | collective-permute-start | bytes 122888 | tf_op jit(solution)/shard_map/ppermute | solution.py:227
  586.2 13.1 %collective-permute-start.37 = (bf16[1,2,2,1,112,640]{5,4,3,2,1,0:T(8,128)(2,1)}, bf16[1,2,2,1,112,640]{5,4,3,2,1,0:T(8,128)(2,1)}, u32[]{:S(2)}, u32[]{:S(2)}) collective-permute-start(bf16[1,2,2,1,112,640]{5,4,3,2,1,0:T(8,128)(2,1)} %copy.117), channel_id=1, source_target_pairs={{0,8},{8,0},{1,9},{9,1},{2,10},{10,2},{3,11},{11,3},{4,12},{12,4},... | collective-permute-start | bytes 1720328 | tf_op jit(solution)/shard_map/ppermute | solution.py:224
  594.0 12.4 %collective-permute-start.39 = (bf16[1,2,2,1,112,640]{5,4,3,2,1,0:T(8,128)(2,1)}, bf16[1,2,2,1,112,640]{5,4,3,2,1,0:T(8,128)(2,1)}, u32[]{:S(2)}, u32[]{:S(2)}) collective-permute-start(bf16[1,2,2,1,112,640]{5,4,3,2,1,0:T(8,128)(2,1)} %copy.121), channel_id=1, source_target_pairs={{0,1},{1,0},{2,3},{3,2},{4,5},{5,4},{6,7},{7,6},{8,9},{9,8},{10,11... | collective-permute-start | bytes 1720328 | tf_op jit(solution)/shard_map/ppermute | solution.py:227
  612.9 33.3 %collective-permute-start.44 = (bf16[3,64,640]{2,1,0:T(8,128)(2,1)}, bf16[3,64,640]{2,1,0:T(8,128)(2,1)}, u32[]{:S(2)}, u32[]{:S(2)}) collective-permute-start(bf16[3,64,640]{2,1,0:T(8,128)(2,1)} %bitcast.133), channel_id=1, source_target_pairs={{0,16},{16,0},{1,17},{17,1},{2,18},{18,2},{3,19},{19,3},{4,20},{20... | collective-permute-start | bytes 737288 | tf_op jit(solution)/shard_map/ppermute | solution.py:40
  615.3 10.6 %collective-permute-start.57 = (bf16[1,2,1,1,112,640]{4,5,3,2,1,0:T(8,128)(2,1)S(1)}, bf16[1,2,1,1,112,640]{4,5,3,2,1,0:T(8,128)(2,1)S(1)}, u32[]{:S(2)}, u32[]{:S(2)}) collective-permute-start(bf16[1,2,1,1,112,640]{4,5,3,2,1,0:T(8,128)(2,1)S(1)} %broadcast_select_fusion.28), channel_id=1, source_target_pairs={{0,2},{1,3},{2,0},{3,1},{4,6},{5,7},{6,4},{7,5},{8,10},{9,11},{10,... | collective-permute-start | bytes 860168 | tf_op jit(solution)/shard_map/ppermute | solution.py:227
  616.2 33.4 %collective-permute-start.45 = (bf16[16,56,640]{2,1,0:T(8,128)(2,1)S(1)}, bf16[16,56,640]{2,1,0:T(8,128)(2,1)S(1)}, u32[]{:S(2)}, u32[]{:S(2)}) collective-permute-start(bf16[16,56,640]{2,1,0:T(8,128)(2,1)S(1)} %broadcast_select_fusion.12), channel_id=1, source_target_pairs={{0,16},{16,0},{1,17},{17,1},{2,18},{18,2},{3,19},{19,3},{4,20},{20... | collective-permute-start | bytes 3440648 | tf_op jit(solution)/shard_map/ppermute | solution.py:40
  616.5 19.5 %collective-permute-start.55 = (bf16[1,2,1,1,112,640]{4,5,3,2,1,0:T(8,128)(2,1)S(1)}, bf16[1,2,1,1,112,640]{4,5,3,2,1,0:T(8,128)(2,1)S(1)}, u32[]{:S(2)}, u32[]{:S(2)}) collective-permute-start(bf16[1,2,1,1,112,640]{4,5,3,2,1,0:T(8,128)(2,1)S(1)} %broadcast_select_fusion.29), channel_id=1, source_target_pairs={{0,2},{1,3},{2,0},{3,1},{4,6},{5,7},{6,4},{7,5},{8,10},{9,11},{10,... | collective-permute-start | bytes 860168 | tf_op jit(solution)/shard_map/ppermute | solution.py:227
  625.9 10.4 %collective-permute-start.58 = (bf16[1,1,1,1,112,640]{4,5,3,2,1,0:T(8,128)(2,1)S(1)}, bf16[1,1,1,1,112,640]{4,5,3,2,1,0:T(8,128)(2,1)S(1)}, u32[]{:S(2)}, u32[]{:S(2)}) collective-permute-start(bf16[1,1,1,1,112,640]{4,5,3,2,1,0:T(8,128)(2,1)S(1)} %broadcast_select_fusion.45), channel_id=1, source_target_pairs={{0,4},{1,5},{2,6},{3,7},{4,0},{5,1},{6,2},{7,3},{8,12},{9,13},{10,... | collective-permute-start | bytes 430088 | tf_op jit(solution)/shard_map/ppermute | solution.py:227
  636.0 9.8 %collective-permute-start.56 = (bf16[1,1,1,1,112,640]{4,5,3,2,1,0:T(8,128)(2,1)S(1)}, bf16[1,1,1,1,112,640]{4,5,3,2,1,0:T(8,128)(2,1)S(1)}, u32[]{:S(2)}, u32[]{:S(2)}) collective-permute-start(bf16[1,1,1,1,112,640]{4,5,3,2,1,0:T(8,128)(2,1)S(1)} %broadcast_select_fusion.46), channel_id=1, source_target_pairs={{0,4},{1,5},{2,6},{3,7},{4,0},{5,1},{6,2},{7,3},{8,12},{9,13},{10,... | collective-permute-start | bytes 430088 | tf_op jit(solution)/shard_map/ppermute | solution.py:227
  646.2 1.9 collective-permute-start.59
  650.2 8.4 %collective-permute-start.50 = (bf16[1,2,2,2,24,640]{5,4,3,2,1,0:T(8,128)(2,1)S(1)}, bf16[1,2,2,2,24,640]{5,4,3,2,1,0:T(8,128)(2,1)S(1)}, u32[]{:S(2)}, u32[]{:S(2)}) collective-permute-start(bf16[1,2,2,2,24,640]{5,4,3,2,1,0:T(8,128)(2,1)S(1)} %bitcast.414), channel_id=1, source_target_pairs={{0,8},{8,0},{1,9},{9,1},{2,10},{10,2},{3,11},{11,3},{4,12},{12,4},... | collective-permute-start | bytes 737288 | tf_op jit(solution)/shard_map/ppermute | solution.py:224
  650.6 9.9 %collective-permute-start.46 = (bf16[2,2,2,1,32,640]{5,4,3,2,1,0:T(8,128)(2,1)S(1)}, bf16[2,2,2,1,32,640]{5,4,3,2,1,0:T(8,128)(2,1)S(1)}, u32[]{:S(2)}, u32[]{:S(2)}) collective-permute-start(bf16[2,2,2,1,32,640]{5,4,3,2,1,0:T(8,128)(2,1)S(1)} %broadcast_select_fusion.26), channel_id=1, source_target_pairs={{0,1},{1,0},{2,3},{3,2},{4,5},{5,4},{6,7},{7,6},{8,9},{9,8},{10,11... | collective-permute-start | bytes 983048 | tf_op jit(solution)/shard_map/ppermute | solution.py:227
  658.7 5.0 collective-permute-start.51
  663.7 4.3 collective-permute-start.52
  663.8 5.4 collective-permute-start.47
  669.3 4.5 collective-permute-start.48
  671.4 5.2 collective-permute-start.53
  673.8 5.0 collective-permute-start.49
  678.9 1.3 collective-permute-start.54
  (180 other events, 2177.8 us)
Sparse Core Ops, SparseCore 0:
  139.7 51.1 all-gather.5
  284.1 45.5 all-gather.3
  369.2 73.5 reduce-scatter.2
  522.6 74.3 reduce-scatter.4
